TPU v7x, 256 devices: a whole 4x4x8 slice. The times are simulated.
256 devices in a mesh: az: 16 (over y_hi, z), ax: 4 (over x), obs: 4 (over y_lo, core).
Axes of the slice: x: 4, y: 4 (y_hi: 2, y_lo: 2; y = y_hi * 2 + y_lo), z: 8, core: 2. Of those that a mesh axis runs over, the one named last changes fastest.
Arguments:
- thickness: bfloat16 [1024, 128, 512], P('az', 'ax'), may hold values from -6 to 6
- loading: bfloat16 [1024, 128, 512], P('az', 'ax'), may hold values from -6 to 6
- kept_modes: int32 [64], replicated, may hold values from 0 to 511
- cap_stations: int32 [8], replicated, may hold values from 64 to 128
- observer_ids: int32 [1024], replicated, may hold values from 0 to 2047
Outputs:
- pressure: float32 [1024, 256], P(('az', 'obs'), 'ax')
All inputs are finite; a program needn't handle non-finite values.
Results may differ from a plain program's by a relative error of at most 0.0055.
Values may be sent and summed in bfloat16 or wider, within the bound.
No kernel may reach another device: no remote copies, remote signals or barrier semaphores. Data moves between devices by JAX's collectives and lax.ppermute only.
A program may use at most 128 MiB of HBM per device.

v0:
```python
import math

import jax
import jax.numpy as jnp
from jax import lax
from jax.sharding import PartitionSpec as P

FREQS = 128
MODES = 64


SPACING = 0.1
RADIUS = 1.0
ARC = 10.0
KMAX = 6.0


def time_table(samples, first_bin, bin_count):
    steps = jnp.arange(samples, dtype=jnp.int32)
    bins = first_bin + jnp.arange(bin_count, dtype=jnp.int32) + 1
    angle = 2.0 * jnp.pi / samples * (steps[:, None] * bins[None, :] % samples).astype(jnp.float32)
    window = 0.5 - 0.5 * jnp.cos(2.0 * jnp.pi / samples * steps.astype(jnp.float32))
    factor = 2.0 / math.sqrt(samples)
    basis = (
        jnp.concatenate(
            [window[:, None] * jnp.cos(angle), -window[:, None] * jnp.sin(angle)], axis=1
        )
        * factor
    )
    return basis.astype(jnp.bfloat16)


def mode_tables(positions, modes, total_az):
    angle = (
        2.0
        * jnp.pi
        / total_az
        * (positions[:, None] * modes[None, :] % total_az).astype(jnp.float32)
    )
    factor = 1.0 / math.sqrt(total_az)
    return (
        (jnp.cos(angle) * factor).astype(jnp.bfloat16),
        (jnp.sin(angle) * factor).astype(jnp.bfloat16),
    )


def combine(cosine_part, sine_part):
    return jnp.stack(
        [
            cosine_part[:, :, 0] + sine_part[:, :, 1],
            cosine_part[:, :, 1] - sine_part[:, :, 0],
            cosine_part[:, :, 2] + sine_part[:, :, 3],
            cosine_part[:, :, 3] - sine_part[:, :, 2],
        ],
        axis=2,
    )


def to_modes(spectrum, mode_cos, mode_sin):
    cosine_part = jnp.einsum(
        "am,azcf->mzcf", mode_cos, spectrum, preferred_element_type=jnp.float32
    )
    sine_part = jnp.einsum("am,azcf->mzcf", mode_sin, spectrum, preferred_element_type=jnp.float32)
    return combine(cosine_part, sine_part)


def cap_weight(panel_index, stations):
    closed = (panel_index[:, None] < stations[None, :]).astype(jnp.float32)
    return jnp.sum(closed, axis=1) / stations.shape[0]


def pressure_term(observer_ids, total_z, panel_index, weight, modal, modes, total_freqs):
    polar = (observer_ids // 64).astype(jnp.float32)
    azimuth_index = observer_ids % 64
    theta = (20.0 + polar * (140.0 / 31.0)) * (jnp.pi / 180.0)
    axial_obs = 0.5 * SPACING * total_z + ARC * jnp.cos(theta)
    radial = ARC * jnp.sin(theta)
    axial_panel = (panel_index.astype(jnp.float32) + 0.5) * SPACING
    distance = jnp.sqrt(
        (axial_obs[:, None] - axial_panel[None, :]) ** 2 + radial[:, None] ** 2 + RADIUS * RADIUS
    )
    inverse = 1.0 / distance
    radial_ratio = (radial[:, None] * inverse)[:, :, None]
    scaled = (inverse * weight[None, :])[:, :, None]
    inverse_three = inverse[:, :, None]
    mode_angle = (
        2.0 * jnp.pi / 64.0 * (modes[None, :] * azimuth_index[:, None] % 64).astype(jnp.float32)
    )
    mode_cos = jnp.cos(mode_angle)[:, :, None]
    mode_sin = jnp.sin(mode_angle)[:, :, None]
    mode_count = modes.shape[0]
    block_width = min(32, total_freqs)
    reals = []
    imags = []
    for block_start in range(0, total_freqs, block_width):
        block_data = modal[:, :, :, block_start : block_start + block_width].astype(jnp.float32)
        wave = (
            KMAX
            * (jnp.arange(block_width, dtype=jnp.int32) + block_start + 1).astype(jnp.float32)
            / total_freqs
        )
        phase = distance[:, :, None] * wave[None, None, :]
        green_re = jnp.cos(phase) * scaled
        green_im = -jnp.sin(phase) * scaled
        thick_re = -wave * green_im
        thick_im = wave * green_re
        load_re = radial_ratio * (green_re * inverse_three - wave * green_im)
        load_im = radial_ratio * (wave * green_re + green_im * inverse_three)
        kernel = jnp.concatenate([thick_re, thick_im, load_re, load_im], axis=1)
        q_re = block_data[:, :, 0]
        q_im = block_data[:, :, 1]
        l_re = block_data[:, :, 2]
        l_im = block_data[:, :, 3]
        column_re = jnp.concatenate([q_re, -q_im, l_re, -l_im], axis=1)
        column_im = jnp.concatenate([q_im, q_re, l_im, l_re], axis=1)
        source = jnp.concatenate([column_re, column_im], axis=0)
        sums = jnp.einsum("okf,nkf->onf", kernel, source, precision=lax.Precision.HIGHEST)
        sum_re = sums[:, :mode_count]
        sum_im = sums[:, mode_count:]
        reals.append(jnp.sum(mode_cos * sum_re - mode_sin * sum_im, axis=1))
        imags.append(jnp.sum(mode_cos * sum_im + mode_sin * sum_re, axis=1))
    return jnp.concatenate([jnp.concatenate(reals, axis=1), jnp.concatenate(imags, axis=1)], axis=1)


def shards(thickness, loading, kept_modes, cap_stations, observer_ids):
    az_rows, z_rows, samples = thickness.shape
    az_count = lax.axis_size("az")
    ax_count = lax.axis_size("ax")
    obs_count = lax.axis_size("obs")
    total_az = az_rows * az_count
    total_z = z_rows * ax_count
    mode_rows = MODES // az_count
    bin_count = FREQS
    first_bin = 0
    basis = time_table(samples, first_bin, bin_count)

    def transform_field(field):
        flat = jnp.dot(
            field.reshape(az_rows * z_rows, samples), basis, preferred_element_type=jnp.float32
        )
        return flat.reshape(az_rows, z_rows, 2, bin_count)

    spectrum = jnp.concatenate(
        [transform_field(thickness), transform_field(loading)], axis=2
    ).astype(jnp.bfloat16)
    mode_cos, mode_sin = mode_tables(jnp.arange(total_az, dtype=jnp.int32), kept_modes, total_az)
    modal_block = to_modes(
        lax.all_to_all(spectrum, "az", split_axis=1, concat_axis=0, tiled=True), mode_cos, mode_sin
    ).astype(jnp.bfloat16)
    modal_data = lax.all_to_all(modal_block, "az", split_axis=0, concat_axis=1, tiled=True)
    modes_here = lax.dynamic_slice_in_dim(kept_modes, lax.axis_index("az") * mode_rows, mode_rows)
    panel_index = lax.axis_index("ax") * z_rows + jnp.arange(z_rows, dtype=jnp.int32)
    weight = cap_weight(panel_index, cap_stations)
    per_block = observer_ids.shape[0] // (az_count * obs_count)
    grouped = observer_ids.reshape(az_count, obs_count, per_block)
    group_ids = lax.dynamic_slice_in_dim(grouped, lax.axis_index("obs"), 1, 1).reshape(
        az_count * per_block
    )
    partial_value = pressure_term(
        group_ids, total_z, panel_index, weight, modal_data, modes_here, FREQS
    )
    partial_value = partial_value * (1.0 / math.sqrt(total_z * MODES))
    row_sums = lax.psum_scatter(partial_value, "az", scatter_dimension=0, tiled=True)
    return lax.psum_scatter(row_sums, "ax", scatter_dimension=1, tiled=True)


def solution(mesh):
    return jax.shard_map(
        shards,
        mesh=mesh,
        in_specs=(P("az", "ax", None), P("az", "ax", None), P(), P(), P()),
        out_specs=P(("az", "obs"), "ax"),
        check_vma=False,
    )
```

profile of v0, /device:TPU:2, one launch (start us, length us, event | category | flops | bytes accessed | tf_op | source)
XLA Modules:
  0.0 353.3 jit_solution(4242799683418392284)
XLA Ops:
  6.5 0.0 copy-start
  6.6 1.1 cosine_multiply_fusion
  7.7 0.0 copy-start.4
  7.7 0.5 copy-done
  8.1 0.2 copy-done.4
  8.4 0.8 fusion.8
  9.1 1.3 copy.53
  10.5 2.1 reshape.427
  12.6 2.5 fusion.9
  15.1 1.3 copy.54
  16.4 1.3 reshape.429
  17.7 3.2 pad_maximum_fusion.4
  21.0 0.0 copy-start.5
  21.0 0.0 copy-start.6
  21.0 2.4 copy.55
  23.5 11.2 %all-to-all-start = ((bf16[64,32,4,128]{3,2,0,1:T(4,128)(2,1)}), bf16[64,32,4,128]{3,2,0,1:T(4,128)(2,1)}, u32[]{:S(2)}, u32[]{:S(2)}) async-start(bf16[64,32,4,128]{3,2,0,1:T(4,128)(2,1)} %copy.55), calls=%async_computation | async-start | bytes 4194304 | tf_op jit(solution)/shard_map/all_to_all | solution.py:148
  34.7 0.0 copy-done.5
  34.7 0.1 reshape.424
  34.9 0.1 reshape.425
  35.0 0.0 copy-done.6
  35.0 0.1 convert_reduce_fusion
  35.1 0.1 sine_multiply_fusion.1
  35.2 0.1 fusion.158
  35.3 17.4 %fusion.52 = (f32[256,32,32]{0,2,1:T(8,128)S(1)}, f32[256,32,32]{0,2,1:T(8,128)S(1)}, f32[256,32,32]{0,2,1:T(8,128)S(1)}, f32[256,32,32]{0,2,1:T(8,128)}, f32[25...) fusion(f32[32]{0:T(128)S(1)} %get-tuple-element.88, ...), kind=kLoop, calls=%fused_computation.59 | loop fusion | flops 13631488 | bytes 16909312 | tf_op jit(solution)/shard_map/mul | solution.py:107
  52.7 2.5 pad_maximum_fusion.2
  55.2 2.6 pad_maximum_fusion.1
  57.8 2.5 pad_maximum_fusion
  60.3 24.9 %all-to-all-done = bf16[64,32,4,128]{3,2,0,1:T(4,128)(2,1)} async-done(((bf16[64,32,4,128]{3,2,0,1:T(4,128)(2,1)}), bf16[64,32,4,128]{3,2,0,1:T(4,128)(2,1)}, u32[]{:S(2)}, u32[]{:S(2)}) %all-to-all-start) | async-done | bytes 2097184 | tf_op jit(solution)/shard_map/all_to_all | solution.py:148
  85.2 2.1 copy.56
  87.4 0.2 copy.57
  87.6 0.0 copy-done.7
  87.6 1.3 fusion.84
  89.0 1.3 fusion.87
  90.4 0.7 copy.58
  91.1 5.7 %all-to-all-start.1 = ((bf16[64,2,4,128]{3,2,1,0:T(4,128)(2,1)}), bf16[64,2,4,128]{3,2,1,0:T(4,128)(2,1)S(1)}, u32[]{:S(2)}, u32[]{:S(2)}) async-start(bf16[64,2,4,128]{3,2,1,0:T(4,128)(2,1)} %copy.58), calls=%async_computation.1 | async-start | bytes 262144 | tf_op jit(solution)/shard_map/all_to_all | solution.py:150
  96.8 0.0 reduce-scatter.7.cloned.1.call-start
  96.8 4.4 %pad_maximum_fusion.3 = f32[256,128,32]{0,2,1:T(8,128)} fusion(f32[256,32,32]{0,2,1:T(8,128)S(1)} %get-tuple-element.61, f32[256,32,32]{0,2,1:T(8,128)} %get-tuple-element.62, f32[256,32,32]{0,2,1:T(8,128)} %get-tuple-element.71, f32[256,32,32]{0,2,1:T(8,128)} %get-tuple-element.70), kind=kLoop, calls=%fused_computation.3 | loop fusion | flops 3145728 | bytes 8388608 | tf_op jit(solution)/shard_map/concatenate | solution.py:109
  101.2 0.1 dynamic_slice.6
  101.3 0.1 fusion.165
  101.4 5.6 %all-to-all-done.1 = bf16[64,2,4,128]{3,2,1,0:T(4,128)(2,1)S(1)} async-done(((bf16[64,2,4,128]{3,2,1,0:T(4,128)(2,1)}), bf16[64,2,4,128]{3,2,1,0:T(4,128)(2,1)S(1)}, u32[]{:S(2)}, u32[]{:S(2)}) %all-to-all-start.1) | async-done | bytes 131104 | tf_op jit(solution)/shard_map/all_to_all | solution.py:150
  107.0 0.1 copy.59
  107.1 0.2 fusion.198
  107.3 0.1 copy.77
  107.6 0.1 copy.76
  107.8 0.1 copy.75
  108.1 0.1 copy.78
  108.2 0.0 copy-start.2
  108.3 0.0 copy-start.1
  108.3 7.2 %fusion.16 = f32[256,8,32]{0,1,2:T(8,128)S(1)} fusion(f32[256,128,32]{0,2,1:T(8,128)} %pad_maximum_fusion.2, f32[4,32,32]{1,0,2:T(4,128)S(1)} %get-tuple-element.29, f32[4,32,32]{1,0,2:T(4,128)S(1)} %get-tuple-element.28, f32[4,32,32]{1,0,2:T(4,128)S(1)} %get-tuple-element.30, f32[4,32,32]{1,0,2:T(4,128)S(1)} %get-tuple-element.27, ...), kind=kOutput, calls=%fused_computation.27 | convolution fusion | flops 100892672 | bytes 4554752 | tf_op jit(solution)/shard_map/okf,nkf->onf/dot_general | solution.py:117
  115.6 0.0 copy-done.2
  115.6 0.0 copy-start.3
  115.6 4.4 %fusion.13 = f32[256,8,32]{0,1,2:T(8,128)S(1)} fusion(f32[256,128,32]{0,2,1:T(8,128)S(1)} %copy-done.2, f32[4,32,32]{1,0,2:T(4,128)S(1)} %get-tuple-element.35, f32[4,32,32]{1,0,2:T(4,128)S(1)} %get-tuple-element.34, f32[4,32,32]{1,0,2:T(4,128)S(1)} %get-tuple-element.36, f32[4,32,32]{1,0,2:T(4,128)S(1)} %get-tuple-element.33, ...), kind=kOutput, calls=%fused_computation.26 | convolution fusion | flops 100892672 | bytes 4554752 | tf_op jit(solution)/shard_map/okf,nkf->onf/dot_general | solution.py:117
  120.0 0.0 copy-done.1
  120.0 4.4 %fusion.10 = f32[256,8,32]{0,1,2:T(8,128)S(1)} fusion(f32[256,128,32]{0,2,1:T(8,128)S(1)} %copy-done.1, f32[4,32,32]{1,0,2:T(4,128)S(1)} %get-tuple-element.41, f32[4,32,32]{1,0,2:T(4,128)S(1)} %get-tuple-element.40, f32[4,32,32]{1,0,2:T(4,128)S(1)} %get-tuple-element.42, f32[4,32,32]{1,0,2:T(4,128)S(1)} %get-tuple-element.39, ...), kind=kOutput, calls=%fused_computation.25 | convolution fusion | flops 100892672 | bytes 4554752 | tf_op jit(solution)/shard_map/okf,nkf->onf/dot_general | solution.py:117
  124.5 4.7 %fusion.19 = f32[256,8,32]{0,1,2:T(8,128)S(1)} fusion(f32[256,128,32]{0,2,1:T(8,128)S(1)} %copy-done.3, f32[4,32,32]{1,0,2:T(4,128)S(1)} %get-tuple-element.47, f32[4,32,32]{1,0,2:T(4,128)S(1)} %get-tuple-element.46, f32[4,32,32]{1,0,2:T(4,128)S(1)} %get-tuple-element.48, f32[4,32,32]{1,0,2:T(4,128)S(1)} %get-tuple-element.45, ...), kind=kOutput, calls=%fused_computation.28 | convolution fusion | flops 100892672 | bytes 4554752 | tf_op jit(solution)/shard_map/okf,nkf->onf/dot_general | solution.py:117
  129.2 0.9 add_reduce_fusion
  130.2 0.8 copy.71
  131.0 0.0 reduce-scatter.7.cloned.1.call-update
  131.0 0.0 reduce-scatter.9.cloned.1.call-start
  131.1 192.2 %reduce-scatter.7.cloned.1.call-done = f32[16,256]{1,0:T(8,128)} async-done(((f32[256,256]{1,0:T(8,128)}), f32[16,256]{1,0:T(8,128)}) %reduce-scatter.7.cloned.1.call-update) | async-done | bytes 16400 | tf_op jit(solution)/shard_map/reduce_scatter | solution.py:163
  323.3 1.5 copy.73
  324.7 0.0 reduce-scatter.9.cloned.1.call-update
  324.8 20.3 %reduce-scatter.9.cloned.1.call-done = f32[64,16]{1,0:T(8,128)} async-done(((f32[256,16]{1,0:T(8,128)}), f32[64,16]{1,0:T(8,128)}) %reduce-scatter.9.cloned.1.call-update) | async-done | bytes 4112
  345.0 1.4 copy.74
  (36 shorter events, 0.6 us)
Async XLA Ops:
  6.5 1.6 copy-start
  7.7 0.7 copy-start.4
  21.0 13.7 %copy-start.5 = (s32[1024]{0:T(1024)S(1)}, s32[1024]{0:T(1024)}, u32[]{:S(2)}) copy-start(s32[1024]{0:T(1024)} %param.9) | copy-start | bytes 12292
  21.0 14.0 %copy-start.6 = (s32[8]{0:T(128)S(1)}, s32[8]{0:T(128)}, u32[]{:S(2)}) copy-start(s32[8]{0:T(128)} %param.8) | copy-start | bytes 100
  23.5 61.8 %all-to-all-start = ((bf16[64,32,4,128]{3,2,0,1:T(4,128)(2,1)}), bf16[64,32,4,128]{3,2,0,1:T(4,128)(2,1)}, u32[]{:S(2)}, u32[]{:S(2)}) async-start(bf16[64,32,4,128]{3,2,0,1:T(4,128)(2,1)} %copy.55), calls=%async_computation | async-start | bytes 4194304 | tf_op jit(solution)/shard_map/all_to_all | solution.py:148
  60.3 27.3 %copy-start.7 = (s32[64]{0:T(128)S(1)}, s32[64]{0:T(128)}, u32[]{:S(2)}) copy-start(s32[64]{0:T(128)} %param.7) | copy-start | bytes 772
  91.1 15.9 %all-to-all-start.1 = ((bf16[64,2,4,128]{3,2,1,0:T(4,128)(2,1)}), bf16[64,2,4,128]{3,2,1,0:T(4,128)(2,1)S(1)}, u32[]{:S(2)}, u32[]{:S(2)}) async-start(bf16[64,2,4,128]{3,2,1,0:T(4,128)(2,1)} %copy.58), calls=%async_computation.1 | async-start | bytes 262144 | tf_op jit(solution)/shard_map/all_to_all | solution.py:150
  96.8 226.5 %reduce-scatter.7.cloned.1.call-start = ((), (), s32[]{:S(2)}) async-start(), calls=%async_computation.4 | async-start | bytes 278528 | tf_op jit(solution)/shard_map/reduce_scatter | solution.py:163
  108.2 7.3 %copy-start.2 = (f32[256,128,32]{0,2,1:T(8,128)S(1)}, f32[256,128,32]{0,2,1:T(8,128)}, u32[]{:S(2)}) copy-start(f32[256,128,32]{0,2,1:T(8,128)} %pad_maximum_fusion.1) | copy-start | bytes 12582916
  108.3 11.7 %copy-start.1 = (f32[256,128,32]{0,2,1:T(8,128)S(1)}, f32[256,128,32]{0,2,1:T(8,128)}, u32[]{:S(2)}) copy-start(f32[256,128,32]{0,2,1:T(8,128)} %pad_maximum_fusion) | copy-start | bytes 12582916
  115.6 8.9 %copy-start.3 = (f32[256,128,32]{0,2,1:T(8,128)S(1)}, f32[256,128,32]{0,2,1:T(8,128)}, u32[]{:S(2)}) copy-start(f32[256,128,32]{0,2,1:T(8,128)} %pad_maximum_fusion.3) | copy-start | bytes 12582916
  131.0 214.0 %reduce-scatter.9.cloned.1.call-start = ((), (), s32[]{:S(2)}) async-start(), calls=%async_computation.5 | async-start | bytes 163840
Sparse Core Ops, SparseCore 0:
  131.1 192.0 reduce-scatter.6
  325.9 19.0 reduce-scatter.8
where the time goes:
time: 356 us; the launch traced here: 353 us
  waiting for transfers between devices  243 us (68%)
  other arithmetic  35.4 us (10%)
  matrix products  26.7 us (8%)
  local copies, waits for them, and re-layouts  17.4 us (5%)
  starting transfers between devices  17 us (5%)
  between operations  13.9 us (4%)
    reduce_scatter x1, waiting for transfers between devices, shards(): lax.psum_scatter(partial_value, 'az', scatter_dimension=0, tiled=True)  192 us
    all_to_all x1, waiting for transfers between devices, shards(): lax.all_to_all(spectrum, 'az', split_axis=1, concat_axis=0, tiled=True)  24.9 us
    dot_general x4, matrix products, pressure_term(): jnp.einsum('okf,nkf->onf', kernel, source, precision=lax.Precision.HIGHEST)  20.8 us
    unnamed x3, waiting for transfers between devices  20.3 us
    mul x1, other arithmetic, pressure_term(): load_re = radial_ratio * (green_re * inverse_three - wave * green_im)  17.4 us
    concatenate x4, other arithmetic, pressure_term(): kernel = jnp.concatenate([thick_re, thick_im, load_re, load_im], axis=1)  12 us
    all_to_all x1, starting transfers between devices, shards(): lax.all_to_all(spectrum, 'az', split_axis=1, concat_axis=0, tiled=True)  11.2 us
  transfers between devices with their start and end apart: 4, of which 4 were waited for; matrix products, arithmetic and copies ran while one was open for 9% of the time, Pallas kernels for 0%

commit v1 on v0

v1 whole, which is shorter than its diff:
```python
import math

import jax
import jax.numpy as jnp
import numpy as np
from jax import lax
from jax.experimental import pallas as pl
from jax.experimental.pallas import tpu as pltpu
from jax.sharding import PartitionSpec as P

FREQS = 128
MODES = 64
POLARS = 32
ARC_POINTS = 64

SPACING = 0.1
RADIUS = 1.0
ARC = 10.0
KMAX = 6.0


def even_odd_series():
    nodes = np.cos((np.arange(64) + 0.5) * np.pi / 64) * 0.5 + 0.5
    root = np.sqrt(nodes)
    fit = np.polynomial.chebyshev.Chebyshev.fit
    even = fit(nodes, np.cos(np.pi * root), 7, domain=[0, 1]).convert(kind=np.polynomial.Polynomial)
    odd = fit(nodes, np.sin(np.pi * root) / root, 6, domain=[0, 1]).convert(
        kind=np.polynomial.Polynomial
    )
    return (
        [float(c) * 4.0**i for i, c in enumerate(even.coef)],
        [2.0 * float(c) * 4.0**i for i, c in enumerate(odd.coef)],
    )


EVEN, ODD = even_odd_series()


def series(coefficients, square):
    total = jnp.full_like(square, coefficients[-1])
    for c in coefficients[-2::-1]:
        total = total * square + c
    return total


def cos_sin_turns(turns):
    part = turns - jnp.round(turns)
    square = part * part
    return series(EVEN, square), part * series(ODD, square)


def time_table(samples, bin_count):
    steps = np.arange(samples)
    bins = np.arange(bin_count) + 1
    angle = 2.0 * np.pi / samples * (steps[:, None] * bins[None, :] % samples)
    window = 0.5 - 0.5 * np.cos(2.0 * np.pi / samples * steps)
    basis = np.concatenate([window[:, None] * np.cos(angle), -window[:, None] * np.sin(angle)], 1)
    return (basis * (2.0 / math.sqrt(samples))).astype(np.float32).astype(jnp.bfloat16)


def pair_sums(rows):
    row = lax.broadcasted_iota(jnp.int32, (8, 128), 0)
    low4, low2, low1 = (row & 4) == 0, (row & 2) == 0, (row & 1) == 0
    four = [
        jnp.where(low4, rows[i], rows[i + 4])
        + pltpu.roll(jnp.where(low4, rows[i + 4], rows[i]), 4, 0)
        for i in range(4)
    ]
    two = [
        jnp.where(
            low2, four[i] + pltpu.roll(four[i], 6, 0), four[i + 2] + pltpu.roll(four[i + 2], 2, 0)
        )
        for i in range(2)
    ]
    return jnp.where(low1, two[0] + pltpu.roll(two[0], 7, 0), two[1] + pltpu.roll(two[1], 1, 0))


def far_field(
    az_rows,
    z_rows,
    az_count,
    obs_count,
    total_az,
    total_z,
    ids_ref,
    caps_ref,
    modes_ref,
    basis_ref,
    thick_ref,
    load_ref,
    out_ref,
    field,
    spectrum,
    wave,
    green,
    sems,
):
    chunks = sems.shape[1]
    step = az_rows * z_rows // chunks
    copies = []
    for chunk in range(chunks):
        for f, source in enumerate((thick_ref, load_ref)):
            rows = pl.ds(chunk * step, step)
            copy = pltpu.make_async_copy(source.at[rows], field.at[f, rows], sems.at[f, chunk])
            copy.start()
            copies.append((f, chunk, copy))
    az, ax, obs = lax.axis_index("az"), lax.axis_index("ax"), lax.axis_index("obs")

    modes = jnp.concatenate([modes_ref[...], modes_ref[...]], axis=1)
    row = lax.broadcasted_iota(jnp.int32, (128, 128), 0)
    column = lax.broadcasted_iota(jnp.int32, (128, 128), 1)
    quarter = 256 * ((row >> 6) + (column >> 6))
    arc_phase = ((row & 63) * modes & 63) * (1024 // ARC_POINTS) - quarter
    arc, _ = cos_sin_turns(arc_phase.astype(jnp.float32) * (1.0 / 1024))
    turn = ((row & 63) + az * az_rows) * modes & (total_az - 1)
    ring, _ = cos_sin_turns((turn * (1024 // total_az) - quarter).astype(jnp.float32) * (1.0 / 1024))
    ring = (ring * (1.0 / math.sqrt(total_az))).astype(jnp.bfloat16)
    arc_high = arc.astype(jnp.bfloat16)
    arc_low = (arc - arc_high.astype(jnp.float32)).astype(jnp.bfloat16)
    contract = (((1,), (1,)), ((), ()))
    modal = lax.dot_general(arc_high, ring, contract, preferred_element_type=jnp.float32)
    modal += lax.dot_general(arc_low, ring, contract, preferred_element_type=jnp.float32)
    modal = modal.astype(jnp.bfloat16)

    bins = (lax.broadcasted_iota(jnp.int32, (1, 128), 1) + 1).astype(jnp.float32)
    wavenumber = KMAX / FREQS * bins
    panel = lax.broadcasted_iota(jnp.int32, (z_rows, 128), 0) + ax * z_rows
    weight = jnp.zeros((z_rows, 128), jnp.float32)
    for c in range(caps_ref.shape[0]):
        weight += (panel < caps_ref[c]).astype(jnp.float32)
    weight *= 1.0 / (caps_ref.shape[0] * math.sqrt(total_z * MODES))
    axial_panel = (panel.astype(jnp.float32) + 0.5) * SPACING

    def polar_step(p, carry):
        index = jnp.full((8, 128), p, jnp.int32).astype(jnp.float32)
        cos_theta, sin_theta = cos_sin_turns((20.0 + index * (140.0 / 31.0)) * (1.0 / 360.0))
        axial = (0.5 * SPACING * total_z + ARC * cos_theta)[:1]
        radial = (ARC * sin_theta)[:1]
        offset = axial - axial_panel
        distance = jnp.sqrt(offset * offset + (radial * radial + RADIUS * RADIUS))
        inverse = 1.0 / distance
        ratio = radial * inverse
        scaled = inverse * weight
        cos_phase, sin_phase = cos_sin_turns(distance * (wavenumber * (0.5 / math.pi)))
        re = cos_phase * scaled
        im = -sin_phase * scaled
        wave_re = wavenumber * re
        wave_im = wavenumber * im
        green[p, 0] = -wave_im
        green[p, 1] = wave_re
        green[p, 2] = ratio * (re * inverse - wave_im)
        green[p, 3] = ratio * (wave_re + im * inverse)
        return carry

    lax.fori_loop(0, POLARS, polar_step, 0, unroll=2)

    for f, chunk, copy in copies:
        copy.wait()
        rows = pl.ds(chunk * step, step)
        value = jnp.dot(field[f, rows], basis_ref[...], preferred_element_type=jnp.float32)
        spectrum[2 * f, rows] = value[:, :FREQS]
        spectrum[2 * f + 1, rows] = value[:, FREQS:]

    def panel_step(z, carry):
        rows = pl.ds(z, az_rows, stride=z_rows)
        parts = [spectrum[c, rows] for c in range(4)]
        source = jnp.concatenate(
            [
                jnp.concatenate([parts[0], parts[2]], axis=1),
                jnp.concatenate([parts[1], parts[3]], axis=1),
            ],
            axis=0,
        ).astype(jnp.bfloat16)
        value = jnp.dot(modal, source, preferred_element_type=jnp.float32)
        there = pl.ds(z, ARC_POINTS, stride=z_rows)
        wave[0, there] = value[:64, :128]
        wave[1, there] = value[64:, :128]
        wave[2, there] = value[:64, 128:]
        wave[3, there] = value[64:, 128:]
        return carry

    lax.fori_loop(0, z_rows, panel_step, 0, unroll=4)

    lane = lax.broadcasted_iota(jnp.int32, (8, 128), 1)
    per_block = ids_ref.shape[0] // (az_count * obs_count)

    def observer_block(block, carry):
        tops = []
        for half in range(2):
            reals, imags = [], []
            for j in range(8):
                where = ids_ref[(block * obs_count + obs) * per_block + half * 8 + j]
                p, q = where >> 6, where & 63
                rows = pl.ds(pl.multiple_of(q * z_rows, z_rows), z_rows)
                k0, k1, k2, k3 = (green[p, c] for c in range(4))
                w0, w1, w2, w3 = (wave[c, rows] for c in range(4))
                re = (k0 * w0 - k1 * w1) + (k2 * w2 - k3 * w3)
                im = (k0 * w1 + k1 * w0) + (k2 * w3 + k3 * w2)
                reals.append(jnp.sum(re.reshape(z_rows // 8, 8, 128), axis=0))
                imags.append(jnp.sum(im.reshape(z_rows // 8, 8, 128), axis=0))
            tops.append((pair_sums(reals), pair_sums(imags)))
        pieces = []
        for part in range(2):
            first, second = tops[0][part], tops[1][part]
            pieces.append(jnp.where(lane < 64, first, pltpu.roll(second, 64, 1)))
            pieces.append(jnp.where(lane < 64, pltpu.roll(first, 64, 1), second))
        rows = pl.ds(pl.multiple_of(block * 32, 32), 32)
        out_ref[rows] = jnp.concatenate(pieces, axis=0).astype(jnp.bfloat16)
        return carry

    lax.fori_loop(0, az_count, observer_block, 0)


def shards(thickness, loading, kept_modes, cap_stations, observer_ids):
    az_rows, z_rows, samples = thickness.shape
    az_count = lax.axis_size("az")
    ax_count = lax.axis_size("ax")
    obs_count = lax.axis_size("obs")
    total_az = az_rows * az_count
    total_z = z_rows * ax_count
    basis = jnp.asarray(time_table(samples, FREQS))
    chunks = 4
    flat = (az_rows * z_rows, samples)

    def body(*refs):
        far_field(az_rows, z_rows, az_count, obs_count, total_az, total_z, *refs)

    smem = pl.BlockSpec(memory_space=pltpu.SMEM)
    vmem = pl.BlockSpec(memory_space=pltpu.VMEM)
    anywhere = pl.BlockSpec(memory_space=pl.ANY)
    partial_value = pl.pallas_call(
        body,
        out_shape=jax.ShapeDtypeStruct((az_count * ax_count * 8, 128), jnp.bfloat16),
        in_specs=[smem, smem, vmem, vmem, anywhere, anywhere],
        out_specs=vmem,
        scratch_shapes=[
            pltpu.VMEM((2, *flat), jnp.bfloat16),
            pltpu.VMEM((4, az_rows * z_rows, FREQS), jnp.float32),
            pltpu.VMEM((4, ARC_POINTS * z_rows, FREQS), jnp.float32),
            pltpu.VMEM((POLARS, 4, z_rows, FREQS), jnp.float32),
            pltpu.SemaphoreType.DMA((2, chunks)),
        ],
        compiler_params=pltpu.CompilerParams(vmem_limit_bytes=48 * 1024 * 1024),
        name="far_field",
    )(
        observer_ids,
        cap_stations,
        kept_modes.reshape(1, MODES),
        basis,
        thickness.reshape(flat),
        loading.reshape(flat),
    )
    pieces = partial_value.reshape(az_count * ax_count, 8, 128)
    arrived = lax.all_to_all(pieces, ("az", "ax"), split_axis=0, concat_axis=0, tiled=True)
    total = jnp.sum(arrived.astype(jnp.float32), axis=0)
    return jnp.concatenate([total[:, :64], total[:, 64:]], axis=0)


def solution(mesh):
    return jax.shard_map(
        shards,
        mesh=mesh,
        in_specs=(P("az", "ax", None), P("az", "ax", None), P(), P(), P()),
        out_specs=P(("az", "obs"), "ax"),
        check_vma=False,
    )
```

time: 356 us -> 49.2 us (0.14)
  waiting for transfers between devices: 243 us -> 0 us
  other arithmetic: 35.4 us -> 0.67 us
  matrix products: 26.7 us -> 0 us
  blocking collectives: 0 us -> 26.2 us
  starting transfers between devices: 17 us -> 0 us
  Pallas kernels: 0 us -> 15.7 us
  between operations: 13.9 us -> 0.02 us
  local copies, waits for them, and re-layouts: 17.4 us -> 6.2 us
    reduce_scatter x1 -> x0, waiting for transfers between devices: 192 us -> none  [shards(): lax.psum_scatter(partial_value, 'az', scatter_dimension=0, tiled=True)]
    all_to_all x2 -> x0, waiting for transfers between devices: 30.5 us -> none  [the longest x1 24.9 us: shards(): lax.all_to_all(spectrum, 'az', split_axis=1, concat_axis=0, tiled=True)]
    dot_general x8 -> x0, matrix products: 26.7 us -> none  [the longest x4 20.8 us: pressure_term(): jnp.einsum('okf,nkf->onf', kernel, source, precision=lax.Precision.HIGHEST)]
    all_to_all x0 -> x1, blocking collectives: none -> 26.2 us  [shards(): lax.all_to_all(pieces, ('az', 'ax'), split_axis=0, concat_axis=0, tiled=T...]
    unnamed x3 -> x0, waiting for transfers between devices: 20.3 us -> none
    mul x5 -> x0, other arithmetic: 18.6 us -> none  [the longest x1 17.4 us: pressure_term(): load_re = radial_ratio * (green_re * inverse_three - wave * green_im)]
    all_to_all x2 -> x0, starting transfers between devices: 16.9 us -> none  [the longest x1 11.2 us: shards(): lax.all_to_all(spectrum, 'az', split_axis=1, concat_axis=0, tiled=True)]
    pallas_call x0 -> x1, Pallas kernels: none -> 15.7 us  [shards(): pl.pallas_call(body, out_shape=jax.ShapeDtypeStruct((az_count * ax_count...]
  transfers between devices with their start and end apart: 4 -> 0, of which waited for: 4 -> 0; matrix products, arithmetic and copies ran while one was open for 9% -> 0% of each run, Pallas kernels for 0% -> 0%
where the time goes in v1:
time: 49.2 us; the launch traced here: 48.7 us
  blocking collectives  26.2 us (53%)
  Pallas kernels  15.7 us (32%)
  local copies, waits for them, and re-layouts  6.2 us (13%)
  other arithmetic  0.67 us (1%)
    all_to_all x1, blocking collectives, shards(): lax.all_to_all(pieces, ('az', 'ax'), split_axis=0, concat_axis=0, tiled=T...  26.2 us
    pallas_call x1, Pallas kernels, shards(): pl.pallas_call(body, out_shape=jax.ShapeDtypeStruct((az_count * ax_count...  15.7 us
    unnamed x12, local copies, waits for them, and re-layouts  6.13 us

profile of v1, /device:TPU:2, one launch (start us, length us, event | category | flops | bytes accessed | tf_op | source)
XLA Modules:
  0.0 48.7 jit_solution(13863971498451235010)
XLA Ops:
  0.0 0.0 copy-start
  0.0 1.6 %copy-done = bf16[64,32,512]{2,1,0:T(8,128)(2,1)S(1)} copy-done((bf16[64,32,512]{2,1,0:T(8,128)(2,1)S(1)}, bf16[64,32,512]{2,1,0:T(8,128)(2,1)}, u32[]{:S(2)}) %copy-start) | copy-done | bytes 2097176
  1.6 0.0 copy-start.1
  1.6 1.6 %copy-done.1 = bf16[64,32,512]{2,1,0:T(8,128)(2,1)S(1)} copy-done((bf16[64,32,512]{2,1,0:T(8,128)(2,1)S(1)}, bf16[64,32,512]{2,1,0:T(8,128)(2,1)}, u32[]{:S(2)}) %copy-start.1) | copy-done | bytes 2097176
  3.2 0.0 copy-start.2
  3.2 0.9 %copy-done.2 = bf16[512,256]{1,0:T(8,128)(2,1)S(1)} copy-done((bf16[512,256]{1,0:T(8,128)(2,1)S(1)}, bf16[512,256]{1,0:T(8,128)(2,1)}, u32[]{:S(2)}) %copy-start.2) | copy-done | bytes 262168
  4.1 0.0 copy-start.3
  4.1 0.7 %copy-done.3 = s32[1024]{0:T(1024)S(1)} copy-done((s32[1024]{0:T(1024)S(1)}, s32[1024]{0:T(1024)}, u32[]{:S(2)}) %copy-start.3) | copy-done | bytes 4120
  4.8 0.0 copy-start.4
  4.8 0.7 %copy-done.4 = s32[8]{0:T(128)S(1)} copy-done((s32[8]{0:T(128)S(1)}, s32[8]{0:T(128)}, u32[]{:S(2)}) %copy-start.4) | copy-done | bytes 56
  5.5 0.0 copy-start.5
  5.5 0.7 %copy-done.5 = s32[64]{0:T(128)S(1)} copy-done((s32[64]{0:T(128)S(1)}, s32[64]{0:T(128)}, u32[]{:S(2)}) %copy-start.5) | copy-done | bytes 280
  6.1 15.7 %far_field.1 = bf16[512,128]{1,0:T(8,128)(2,1)S(1)} custom-call(s32[1024]{0:T(1024)S(1)} %copy-done.3, s32[8]{0:T(128)S(1)} %copy-done.4, s32[1,64]{1,0:T(1,128)S(1)} %bitcast.7, bf16[512,256]{1,0:T(8,128)(2,1)S(1)} %copy-done.2, bf16[2048,512]{1,0:T(8,128)(2,1)S(1)} %bitcast.4, bf16[2048,512]{1,0:T(8,128)(2,1)S(1)} %bitcast.5), custom_call_target="tpu_custom_call" | custom-call | tf_op jit(solution)/shard_map/far_field/pallas_call | solution.py:231
  21.8 26.2 %all_to_all.5 = bf16[64,8,128]{2,1,0:T(8,128)(2,1)S(1)} all-to-all(bf16[64,8,128]{2,1,0:T(8,128)(2,1)S(1)} %bitcast.6), channel_id=1, replica_groups=mesh['az'=16,'ax'=4,'obs'=4] {'az','ax'}, dimensions={0} | all-to-all | bytes 262144 | tf_op jit(solution)/shard_map/all_to_all | solution.py:254
  47.9 0.1 convert_reduce_fusion
  48.0 0.1 fusion
  48.1 0.6 %pad_maximum_fusion = f32[16,64]{1,0:T(8,128)} fusion(f32[8,64]{1,0:T(8,128)S(1)} %get-tuple-element.6, f32[8,64]{1,0:T(8,128)S(1)} %get-tuple-element.5), kind=kLoop, calls=%fused_computation.1 | loop fusion | flops 1024 | bytes 8192 | tf_op jit(solution)/shard_map/concatenate | solution.py:256
Async XLA Ops:
  0.0 1.6 %copy-start = (bf16[64,32,512]{2,1,0:T(8,128)(2,1)S(1)}, bf16[64,32,512]{2,1,0:T(8,128)(2,1)}, u32[]{:S(2)}) copy-start(bf16[64,32,512]{2,1,0:T(8,128)(2,1)} %param.6) | copy-start | bytes 6291460
  1.6 1.6 %copy-start.1 = (bf16[64,32,512]{2,1,0:T(8,128)(2,1)S(1)}, bf16[64,32,512]{2,1,0:T(8,128)(2,1)}, u32[]{:S(2)}) copy-start(bf16[64,32,512]{2,1,0:T(8,128)(2,1)} %param.7) | copy-start | bytes 6291460
  3.2 0.9 %copy-start.2 = (bf16[512,256]{1,0:T(8,128)(2,1)S(1)}, bf16[512,256]{1,0:T(8,128)(2,1)}, u32[]{:S(2)}) copy-start(bf16[512,256]{1,0:T(8,128)(2,1)} %constant.4.clone.refs_3_) | copy-start | bytes 786436
  4.1 0.7 %copy-start.3 = (s32[1024]{0:T(1024)S(1)}, s32[1024]{0:T(1024)}, u32[]{:S(2)}) copy-start(s32[1024]{0:T(1024)} %refs_0_.1) | copy-start | bytes 12292
  4.8 0.7 %copy-start.4 = (s32[8]{0:T(128)S(1)}, s32[8]{0:T(128)}, u32[]{:S(2)}) copy-start(s32[8]{0:T(128)} %refs_1_.1) | copy-start | bytes 100
  5.5 0.7 %copy-start.5 = (s32[64]{0:T(128)S(1)}, s32[64]{0:T(128)}, u32[]{:S(2)}) copy-start(s32[64]{0:T(128)} %param.8) | copy-start | bytes 772

commit v2 on v1

v2 whole, which is shorter than its diff:
```python
import math

import jax
import jax.numpy as jnp
import numpy as np
from jax import lax
from jax.experimental import pallas as pl
from jax.experimental.pallas import tpu as pltpu
from jax.sharding import PartitionSpec as P

FREQS = 128
MODES = 64
POLARS = 32
ARC_POINTS = 64
STRIDE = 40

SPACING = 0.1
RADIUS = 1.0
ARC = 10.0
KMAX = 6.0


def even_odd_series():
    nodes = np.cos((np.arange(64) + 0.5) * np.pi / 64) * 0.5 + 0.5
    root = np.sqrt(nodes)
    fit = np.polynomial.chebyshev.Chebyshev.fit
    even = fit(nodes, np.cos(np.pi * root), 7, domain=[0, 1]).convert(kind=np.polynomial.Polynomial)
    odd = fit(nodes, np.sin(np.pi * root) / root, 6, domain=[0, 1]).convert(
        kind=np.polynomial.Polynomial
    )
    return (
        [float(c) * 4.0**i for i, c in enumerate(even.coef)],
        [2.0 * float(c) * 4.0**i for i, c in enumerate(odd.coef)],
    )


EVEN, ODD = even_odd_series()


def series(coefficients, square):
    total = jnp.full_like(square, coefficients[-1])
    for c in coefficients[-2::-1]:
        total = total * square + c
    return total


def cos_sin_turns(turns):
    part = turns - jnp.round(turns)
    square = part * part
    return series(EVEN, square), part * series(ODD, square)


def time_table(samples, bin_count):
    steps = np.arange(samples)
    bins = np.arange(bin_count) + 1
    angle = 2.0 * np.pi / samples * (steps[:, None] * bins[None, :] % samples)
    window = 0.5 - 0.5 * np.cos(2.0 * np.pi / samples * steps)
    basis = np.concatenate([window[:, None] * np.cos(angle), -window[:, None] * np.sin(angle)], 1)
    return (basis * (2.0 / math.sqrt(samples))).astype(np.float32).astype(jnp.bfloat16)


def far_field(
    az_rows,
    z_rows,
    az_count,
    obs_count,
    total_az,
    total_z,
    ids_from,
    caps_from,
    modes_from,
    basis_from,
    thick_from,
    load_from,
    out_ref,
    ids_ref,
    caps_ref,
    modes_ref,
    basis_ref,
    field,
    spectrum,
    wave,
    green,
    sums,
    sems,
):
    fetch = [
        pltpu.make_async_copy(source, target, sems.at[i])
        for i, (source, target) in enumerate(
            (
                (caps_from, caps_ref),
                (modes_from, modes_ref),
                (basis_from, basis_ref),
                (thick_from, field.at[0]),
                (load_from, field.at[1]),
                (ids_from, ids_ref),
            )
        )
    ]
    for copy in fetch:
        copy.start()
    az, ax, obs = lax.axis_index("az"), lax.axis_index("ax"), lax.axis_index("obs")

    fetch[0].wait()
    bins = (lax.broadcasted_iota(jnp.int32, (1, 128), 1) + 1).astype(jnp.float32)
    wavenumber = KMAX / FREQS * bins
    panel = lax.broadcasted_iota(jnp.int32, (z_rows, 128), 0) + ax * z_rows
    weight = jnp.zeros((z_rows, 128), jnp.float32)
    for c in range(caps_ref.shape[0]):
        weight += (panel < caps_ref[c]).astype(jnp.float32)
    weight *= 1.0 / (caps_ref.shape[0] * math.sqrt(total_z * MODES))
    axial_panel = (panel.astype(jnp.float32) + 0.5) * SPACING

    def polar_step(p, carry):
        index = jnp.full((8, 128), p, jnp.int32).astype(jnp.float32)
        cos_theta, sin_theta = cos_sin_turns((20.0 + index * (140.0 / 31.0)) * (1.0 / 360.0))
        axial = (0.5 * SPACING * total_z + ARC * cos_theta)[:1]
        radial = (ARC * sin_theta)[:1]
        offset = axial - axial_panel
        distance = jnp.sqrt(offset * offset + (radial * radial + RADIUS * RADIUS))
        inverse = 1.0 / distance
        ratio = radial * inverse
        scaled = inverse * weight
        cos_phase, sin_phase = cos_sin_turns(distance * (wavenumber * (0.5 / math.pi)))
        re = cos_phase * scaled
        im = -sin_phase * scaled
        wave_re = wavenumber * re
        wave_im = wavenumber * im
        green[p, 0] = -wave_im
        green[p, 1] = wave_re
        green[p, 2] = ratio * (re * inverse - wave_im)
        green[p, 3] = ratio * (wave_re + im * inverse)
        return carry

    lax.fori_loop(0, POLARS, polar_step, 0, unroll=2)

    fetch[1].wait()
    modes = jnp.concatenate([modes_ref[...], modes_ref[...]], axis=1)
    row = lax.broadcasted_iota(jnp.int32, (128, 128), 0)
    column = lax.broadcasted_iota(jnp.int32, (128, 128), 1)
    quarter = 256 * ((row >> 6) + (column >> 6))
    arc_phase = ((row & 63) * modes & 63) * (1024 // ARC_POINTS) - quarter
    arc, _ = cos_sin_turns(arc_phase.astype(jnp.float32) * (1.0 / 1024))
    turn = ((row & 63) + az * az_rows) * modes & (total_az - 1)
    ring, _ = cos_sin_turns((turn * (1024 // total_az) - quarter).astype(jnp.float32) * (1.0 / 1024))
    ring = (ring * (1.0 / math.sqrt(total_az))).astype(jnp.bfloat16)
    arc_high = arc.astype(jnp.bfloat16)
    arc_low = (arc - arc_high.astype(jnp.float32)).astype(jnp.bfloat16)
    contract = (((1,), (1,)), ((), ()))
    modal = lax.dot_general(arc_high, ring, contract, preferred_element_type=jnp.float32)
    modal += lax.dot_general(arc_low, ring, contract, preferred_element_type=jnp.float32)
    modal = modal.astype(jnp.bfloat16)

    fetch[2].wait()
    for f in range(2):
        fetch[3 + f].wait()
        value = jnp.dot(field[f], basis_ref[...], preferred_element_type=jnp.float32)
        for i in range(az_rows):
            here = value[i * z_rows : (i + 1) * z_rows]
            there = pl.ds(i * STRIDE, z_rows)
            spectrum[2 * f, there] = here[:, :FREQS]
            spectrum[2 * f + 1, there] = here[:, FREQS:]

    def panel_step(z, carry):
        rows = pl.ds(z, az_rows, stride=STRIDE)
        parts = [spectrum[c, rows] for c in range(4)]
        source = jnp.concatenate(
            [
                jnp.concatenate([parts[0], parts[2]], axis=1),
                jnp.concatenate([parts[1], parts[3]], axis=1),
            ],
            axis=0,
        ).astype(jnp.bfloat16)
        value = jnp.dot(modal, source, preferred_element_type=jnp.float32)
        there = pl.ds(z, ARC_POINTS, stride=STRIDE)
        wave[0, there] = value[:64, :128]
        wave[1, there] = value[64:, :128]
        wave[2, there] = value[:64, 128:]
        wave[3, there] = value[64:, 128:]
        return carry

    lax.fori_loop(0, z_rows, panel_step, 0, unroll=8)

    fetch[5].wait()
    lane = lax.broadcasted_iota(jnp.int32, (8, 128), 1)
    per_block = ids_ref.shape[0] // (az_count * obs_count)

    def observer_step(block, carry):
        for j in range(per_block):
            where = ids_ref[(block * obs_count + obs) * per_block + j]
            p, q = where >> 6, where & 63
            rows = pl.ds(pl.multiple_of(q * STRIDE, 8), z_rows)
            k0, k1, k2, k3 = (green[p, c] for c in range(4))
            w0, w1, w2, w3 = (wave[c, rows] for c in range(4))
            re = (k0 * w0 - k1 * w1) + (k2 * w2 - k3 * w3)
            im = (k0 * w1 + k1 * w0) + (k2 * w3 + k3 * w2)
            there = pl.ds(pl.multiple_of((block * per_block + j) * 8, 8), 8)
            sums[0, there] = jnp.sum(re.reshape(z_rows // 8, 8, 128), axis=0)
            sums[1, there] = jnp.sum(im.reshape(z_rows // 8, 8, 128), axis=0)
        return carry

    lax.fori_loop(0, az_count, observer_step, 0)

    def gather_step(block, carry):
        pieces = []
        for part in range(2):
            halves = []
            for half in range(2):
                first = (block * per_block + half * 8) * 8
                rows = [sums[part, pl.ds(first + i, 8, stride=8)] for i in range(8)]
                while len(rows) > 1:
                    rows = [x + y for x, y in zip(rows[::2], rows[1::2])]
                halves.append(rows[0])
            low, high = halves
            pieces.append(jnp.where(lane < 64, low, pltpu.roll(high, 64, 1)))
            pieces.append(jnp.where(lane < 64, pltpu.roll(low, 64, 1), high))
        rows = pl.ds(pl.multiple_of(block * 32, 32), 32)
        out_ref[rows] = jnp.concatenate(pieces, axis=0).astype(jnp.bfloat16)
        return carry

    lax.fori_loop(0, az_count, gather_step, 0, unroll=2)


def shards(thickness, loading, kept_modes, cap_stations, observer_ids):
    az_rows, z_rows, samples = thickness.shape
    az_count = lax.axis_size("az")
    ax_count = lax.axis_size("ax")
    obs_count = lax.axis_size("obs")
    total_az = az_rows * az_count
    total_z = z_rows * ax_count
    basis = jnp.asarray(time_table(samples, FREQS))
    flat = (az_rows * z_rows, samples)

    def body(*refs):
        far_field(az_rows, z_rows, az_count, obs_count, total_az, total_z, *refs)

    anywhere = pl.BlockSpec(memory_space=pl.ANY)
    partial_value = pl.pallas_call(
        body,
        out_shape=jax.ShapeDtypeStruct((az_count * ax_count * 8, 128), jnp.bfloat16),
        in_specs=[anywhere] * 6,
        out_specs=pl.BlockSpec(memory_space=pltpu.VMEM),
        scratch_shapes=[
            pltpu.SMEM(observer_ids.shape, jnp.int32),
            pltpu.SMEM(cap_stations.shape, jnp.int32),
            pltpu.VMEM((1, MODES), jnp.int32),
            pltpu.VMEM(basis.shape, jnp.bfloat16),
            pltpu.VMEM((2, *flat), jnp.bfloat16),
            pltpu.VMEM((4, az_rows * STRIDE, FREQS), jnp.float32),
            pltpu.VMEM((4, ARC_POINTS * STRIDE, FREQS), jnp.float32),
            pltpu.VMEM((POLARS, 4, z_rows, FREQS), jnp.float32),
            pltpu.VMEM((2, observer_ids.shape[0] // obs_count * 8, FREQS), jnp.float32),
            pltpu.SemaphoreType.DMA((6,)),
        ],
        compiler_params=pltpu.CompilerParams(vmem_limit_bytes=60 * 1024 * 1024),
        name="far_field",
    )(
        observer_ids,
        cap_stations,
        kept_modes.reshape(1, MODES),
        basis,
        thickness.reshape(flat),
        loading.reshape(flat),
    )
    pieces = partial_value.reshape(az_count * ax_count, 8, 128)
    arrived = lax.all_to_all(pieces, ("az", "ax"), split_axis=0, concat_axis=0, tiled=True)
    total = jnp.sum(arrived.astype(jnp.float32), axis=0)
    return jnp.concatenate([total[:, :64], total[:, 64:]], axis=0)


def solution(mesh):
    return jax.shard_map(
        shards,
        mesh=mesh,
        in_specs=(P("az", "ax", None), P("az", "ax", None), P(), P(), P()),
        out_specs=P(("az", "obs"), "ax"),
        check_vma=False,
    )
```

time: 49.2 us -> 38.1 us (0.77)
  local copies, waits for them, and re-layouts: 6.2 us -> 0.07 us
  Pallas kernels: 15.7 us -> 10.5 us
    unnamed x12 -> x0, local copies, waits for them, and re-layouts: 6.13 us -> none
    pallas_call x1, Pallas kernels: 15.7 us -> 10.5 us  [shards(): pl.pallas_call(body, out_shape=jax.ShapeDtypeStruct((az_count * ax_count...]
where the time goes in v2:
time: 38.1 us; the launch traced here: 37.7 us
  blocking collectives  26.4 us (69%)
  Pallas kernels  10.5 us (28%)
  other arithmetic  0.67 us (2%)
    all_to_all x1, blocking collectives, shards(): lax.all_to_all(pieces, ('az', 'ax'), split_axis=0, concat_axis=0, tiled=T...  26.4 us
    pallas_call x1, Pallas kernels, shards(): pl.pallas_call(body, out_shape=jax.ShapeDtypeStruct((az_count * ax_count...  10.5 us

profile of v2, /device:TPU:2, one launch (start us, length us, event | category | flops | bytes accessed | tf_op | source)
XLA Modules:
  0.0 37.7 jit_solution(10858483749572686842)
XLA Ops:
  0.0 10.5 %far_field.1 = bf16[512,128]{1,0:T(8,128)(2,1)} custom-call(s32[1024]{0:T(1024)} %refs_0_.1, s32[8]{0:T(128)} %refs_1_.1, s32[1,64]{1,0:T(1,128)} %bitcast.7, bf16[512,256]{1,0:T(8,128)(2,1)} %constant.4.clone.refs_3_, bf16[2048,512]{1,0:T(8,128)(2,1)} %bitcast.4, bf16[2048,512]{1,0:T(8,128)(2,1)} %bitcast.5), custom_call_target="tpu_custom_call" | custom-call | tf_op jit(solution)/shard_map/far_field/pallas_call | solution.py:238
  10.5 26.4 %all_to_all.5 = bf16[64,8,128]{2,1,0:T(8,128)(2,1)S(1)} all-to-all(bf16[64,8,128]{2,1,0:T(8,128)(2,1)} %bitcast.6), channel_id=1, replica_groups=mesh['az'=16,'ax'=4,'obs'=4] {'az','ax'}, dimensions={0} | all-to-all | bytes 262144 | tf_op jit(solution)/shard_map/all_to_all | solution.py:266
  36.9 0.1 convert_reduce_fusion
  37.0 0.1 fusion
  37.1 0.6 %pad_maximum_fusion = f32[16,64]{1,0:T(8,128)} fusion(f32[8,64]{1,0:T(8,128)S(1)} %get-tuple-element.6, f32[8,64]{1,0:T(8,128)S(1)} %get-tuple-element.5), kind=kLoop, calls=%fused_computation.1 | loop fusion | flops 1024 | bytes 8192 | tf_op jit(solution)/shard_map/concatenate | solution.py:268

commit v3 on v2

--- a/solution.py
+++ b/solution.py
@@ -18,6 +18,27 @@
 RADIUS = 1.0
 ARC = 10.0
 KMAX = 6.0
+
+
+Y_ORDER = (1, 0)
+Z_ORDER = (4, 5, 6, 7, 3, 2, 1, 0)
+AX_ORDER = (2, 3, 1, 0)
+
+
+def exchange_groups(az_count, ax_count, obs_count):
+    z_count = az_count // 2
+    groups = []
+    for twist in range(obs_count // 2):
+        for core in range(2):
+            groups.append(
+                [
+                    ((y * z_count + z) * ax_count + ax) * obs_count + 2 * (twist ^ y) + core
+                    for y in Y_ORDER
+                    for z in Z_ORDER
+                    for ax in AX_ORDER
+                ]
+            )
+    return groups
 
 
 def even_odd_series():
@@ -184,10 +205,17 @@
     fetch[5].wait()
     lane = lax.broadcasted_iota(jnp.int32, (8, 128), 1)
     per_block = ids_ref.shape[0] // (az_count * obs_count)
+    z_count = az_count // 2
+    twist = (obs >> 1) ^ (az // z_count)
 
     def observer_step(block, carry):
+        y = 1 - block // z_count
+        z = block % z_count
+        z = jnp.where(z < z_count // 2, z + z_count // 2, z_count - 1 - z)
+        there_obs = 2 * (twist ^ y) + (obs & 1)
+        first_id = ((y * z_count + z) * obs_count + there_obs) * per_block
         for j in range(per_block):
-            where = ids_ref[(block * obs_count + obs) * per_block + j]
+            where = ids_ref[first_id + j]
             p, q = where >> 6, where & 63
             rows = pl.ds(pl.multiple_of(q * STRIDE, 8), z_rows)
             k0, k1, k2, k3 = (green[p, c] for c in range(4))
@@ -215,7 +243,9 @@
             pieces.append(jnp.where(lane < 64, low, pltpu.roll(high, 64, 1)))
             pieces.append(jnp.where(lane < 64, pltpu.roll(low, 64, 1), high))
         rows = pl.ds(pl.multiple_of(block * 32, 32), 32)
-        out_ref[rows] = jnp.concatenate(pieces, axis=0).astype(jnp.bfloat16)
+        out_ref[rows] = jnp.concatenate([pieces[ax] for ax in AX_ORDER], axis=0).astype(
+            jnp.bfloat16
+        )
         return carry
 
     lax.fori_loop(0, az_count, gather_step, 0, unroll=2)
@@ -263,7 +293,14 @@
         loading.reshape(flat),
     )
     pieces = partial_value.reshape(az_count * ax_count, 8, 128)
-    arrived = lax.all_to_all(pieces, ("az", "ax"), split_axis=0, concat_axis=0, tiled=True)
+    arrived = lax.all_to_all(
+        pieces,
+        ("az", "ax", "obs"),
+        split_axis=0,
+        concat_axis=0,
+        axis_index_groups=exchange_groups(az_count, ax_count, obs_count),
+        tiled=True,
+    )
     total = jnp.sum(arrived.astype(jnp.float32), axis=0)
     return jnp.concatenate([total[:, :64], total[:, 64:]], axis=0)
 

time: 38.1 us -> 31.7 us (0.83)
  blocking collectives: 26.4 us -> 20.1 us
    all_to_all x1, blocking collectives: 26.4 us -> 20.1 us  [shards(): lax.all_to_all(pieces, ('az', 'ax', 'obs'), split_axis=0, concat_axis=0,...]
where the time goes in v3:
time: 31.7 us; the launch traced here: 31.5 us
  blocking collectives  20.1 us (63%)
  Pallas kernels  10.7 us (34%)
  other arithmetic  0.67 us (2%)
    all_to_all x1, blocking collectives, shards(): lax.all_to_all(pieces, ('az', 'ax', 'obs'), split_axis=0, concat_axis=0,...  20.1 us
    pallas_call x1, Pallas kernels, shards(): pl.pallas_call(body, out_shape=jax.ShapeDtypeStruct((az_count * ax_count...  10.7 us

profile of v3, /device:TPU:2, one launch (start us, length us, event | category | flops | bytes accessed | tf_op | source)
XLA Modules:
  0.0 31.5 jit_solution(15624389837361345073)
XLA Ops:
  0.0 10.7 %far_field.1 = bf16[512,128]{1,0:T(8,128)(2,1)} custom-call(s32[1024]{0:T(1024)} %refs_0_.1, s32[8]{0:T(128)} %refs_1_.1, s32[1,64]{1,0:T(1,128)} %bitcast.7, bf16[512,256]{1,0:T(8,128)(2,1)} %constant.4.clone.refs_3_, bf16[2048,512]{1,0:T(8,128)(2,1)} %bitcast.4, bf16[2048,512]{1,0:T(8,128)(2,1)} %bitcast.5), custom_call_target="tpu_custom_call" | custom-call | tf_op jit(solution)/shard_map/far_field/pallas_call | solution.py:268
  10.7 20.1 %all_to_all.5 = bf16[64,8,128]{2,1,0:T(8,128)(2,1)S(1)} all-to-all(bf16[64,8,128]{2,1,0:T(8,128)(2,1)} %bitcast.6), channel_id=1, replica_groups={{202,206,198,194,218,222,214,210,234,238,230,226,250,254,246,242,186,19..., dimensions={0} | all-to-all | bytes 262144 | tf_op jit(solution)/shard_map/all_to_all | solution.py:296
  30.8 0.1 convert_reduce_fusion
  30.8 0.1 fusion
  30.9 0.6 %pad_maximum_fusion = f32[16,64]{1,0:T(8,128)} fusion(f32[8,64]{1,0:T(8,128)S(1)} %get-tuple-element.6, f32[8,64]{1,0:T(8,128)S(1)} %get-tuple-element.5), kind=kLoop, calls=%fused_computation.1 | loop fusion | flops 1024 | bytes 8192 | tf_op jit(solution)/shard_map/concatenate | solution.py:305

commit v4 on v3

--- a/solution.py
+++ b/solution.py
@@ -132,7 +132,7 @@
     weight *= 1.0 / (caps_ref.shape[0] * math.sqrt(total_z * MODES))
     axial_panel = (panel.astype(jnp.float32) + 0.5) * SPACING
 
-    def polar_step(p, carry):
+    def polar_step(p):
         index = jnp.full((8, 128), p, jnp.int32).astype(jnp.float32)
         cos_theta, sin_theta = cos_sin_turns((20.0 + index * (140.0 / 31.0)) * (1.0 / 360.0))
         axial = (0.5 * SPACING * total_z + ARC * cos_theta)[:1]
@@ -151,9 +151,9 @@
         green[p, 1] = wave_re
         green[p, 2] = ratio * (re * inverse - wave_im)
         green[p, 3] = ratio * (wave_re + im * inverse)
-        return carry
-
-    lax.fori_loop(0, POLARS, polar_step, 0, unroll=2)
+
+    for p in range(POLARS):
+        polar_step(p)
 
     fetch[1].wait()
     modes = jnp.concatenate([modes_ref[...], modes_ref[...]], axis=1)
@@ -172,15 +172,20 @@
     modal += lax.dot_general(arc_low, ring, contract, preferred_element_type=jnp.float32)
     modal = modal.astype(jnp.bfloat16)
 
-    fetch[2].wait()
+    for copy in fetch[2:5]:
+        copy.wait()
     for f in range(2):
-        fetch[3 + f].wait()
-        value = jnp.dot(field[f], basis_ref[...], preferred_element_type=jnp.float32)
-        for i in range(az_rows):
-            here = value[i * z_rows : (i + 1) * z_rows]
-            there = pl.ds(i * STRIDE, z_rows)
-            spectrum[2 * f, there] = here[:, :FREQS]
-            spectrum[2 * f + 1, there] = here[:, FREQS:]
+        for first in range(0, az_rows, 8):
+            value = jnp.dot(
+                field[f, first * z_rows : (first + 8) * z_rows],
+                basis_ref[...],
+                preferred_element_type=jnp.float32,
+            )
+            for i in range(8):
+                here = value[i * z_rows : (i + 1) * z_rows]
+                there = pl.ds((first + i) * STRIDE, z_rows)
+                spectrum[2 * f, there] = here[:, :FREQS]
+                spectrum[2 * f + 1, there] = here[:, FREQS:]
 
     def panel_step(z, carry):
         rows = pl.ds(z, az_rows, stride=STRIDE)
@@ -227,7 +232,7 @@
             sums[1, there] = jnp.sum(im.reshape(z_rows // 8, 8, 128), axis=0)
         return carry
 
-    lax.fori_loop(0, az_count, observer_step, 0)
+    lax.fori_loop(0, az_count, observer_step, 0, unroll=2)
 
     def gather_step(block, carry):
         pieces = []
@@ -248,7 +253,7 @@
         )
         return carry
 
-    lax.fori_loop(0, az_count, gather_step, 0, unroll=2)
+    lax.fori_loop(0, az_count, gather_step, 0, unroll=8)
 
 
 def shards(thickness, loading, kept_modes, cap_stations, observer_ids):

time: 31.7 us -> 29.7 us (0.937)
  Pallas kernels: 10.7 us -> 8.74 us
    pallas_call x1, Pallas kernels: 10.7 us -> 8.74 us  [shards(): pl.pallas_call(body, out_shape=jax.ShapeDtypeStruct((az_count * ax_count...]
where the time goes in v4:
time: 29.7 us; the launch traced here: 29.6 us
  blocking collectives  20.1 us (68%)
  Pallas kernels  8.74 us (29%)
  other arithmetic  0.67 us (2%)
    all_to_all x1, blocking collectives, shards(): lax.all_to_all(pieces, ('az', 'ax', 'obs'), split_axis=0, concat_axis=0,...  20.1 us
    pallas_call x1, Pallas kernels, shards(): pl.pallas_call(body, out_shape=jax.ShapeDtypeStruct((az_count * ax_count...  8.74 us
    concatenate x1, other arithmetic, shards(): return jnp.concatenate([total[:, :64], total[:, 64:]], axis=0)  0.6 us

profile of v4, /device:TPU:2, one launch (start us, length us, event | category | flops | bytes accessed | tf_op | source)
XLA Modules:
  0.0 29.6 jit_solution(10070556018471180345)
XLA Ops:
  0.0 8.7 %far_field.1 = bf16[512,128]{1,0:T(8,128)(2,1)} custom-call(s32[1024]{0:T(1024)} %refs_0_.1, s32[8]{0:T(128)} %refs_1_.1, s32[1,64]{1,0:T(1,128)} %bitcast.7, bf16[512,256]{1,0:T(8,128)(2,1)} %constant.4.clone.refs_3_, bf16[2048,512]{1,0:T(8,128)(2,1)} %bitcast.4, bf16[2048,512]{1,0:T(8,128)(2,1)} %bitcast.5), custom_call_target="tpu_custom_call" | custom-call | tf_op jit(solution)/shard_map/far_field/pallas_call | solution.py:273
  8.8 20.1 %all_to_all.5 = bf16[64,8,128]{2,1,0:T(8,128)(2,1)S(1)} all-to-all(bf16[64,8,128]{2,1,0:T(8,128)(2,1)} %bitcast.6), channel_id=1, replica_groups={{202,206,198,194,218,222,214,210,234,238,230,226,250,254,246,242,186,19..., dimensions={0} | all-to-all | bytes 262144 | tf_op jit(solution)/shard_map/all_to_all | solution.py:301
  28.8 0.1 convert_reduce_fusion
  28.9 0.1 fusion
  29.0 0.6 %pad_maximum_fusion = f32[16,64]{1,0:T(8,128)} fusion(f32[8,64]{1,0:T(8,128)S(1)} %get-tuple-element.6, f32[8,64]{1,0:T(8,128)S(1)} %get-tuple-element.5), kind=kLoop, calls=%fused_computation.1 | loop fusion | flops 1024 | bytes 8192 | tf_op jit(solution)/shard_map/concatenate | solution.py:310

commit v5 on v4

--- a/solution.py
+++ b/solution.py
@@ -232,7 +232,7 @@
             sums[1, there] = jnp.sum(im.reshape(z_rows // 8, 8, 128), axis=0)
         return carry
 
-    lax.fori_loop(0, az_count, observer_step, 0, unroll=2)
+    lax.fori_loop(0, az_count, observer_step, 0, unroll=4)
 
     def gather_step(block, carry):
         pieces = []
@@ -272,7 +272,7 @@
     anywhere = pl.BlockSpec(memory_space=pl.ANY)
     partial_value = pl.pallas_call(
         body,
-        out_shape=jax.ShapeDtypeStruct((az_count * ax_count * 8, 128), jnp.bfloat16),
+        out_shape=pltpu.VMEM((az_count * ax_count * 8, 128), jnp.bfloat16),
         in_specs=[anywhere] * 6,
         out_specs=pl.BlockSpec(memory_space=pltpu.VMEM),
         scratch_shapes=[

time: 29.7 us -> 28.7 us (0.966)
  Pallas kernels: 8.74 us -> 8.02 us
  blocking collectives: 20.1 us -> 19.8 us
    pallas_call x1, Pallas kernels: 8.74 us -> 8.02 us  [shards(): pl.pallas_call(body, out_shape=pltpu.VMEM((az_count * ax_count * 8, 128),...]
where the time goes in v5:
time: 28.7 us; the launch traced here: 28.6 us
  blocking collectives  19.8 us (69%)
  Pallas kernels  8.02 us (28%)
  other arithmetic  0.67 us (2%)
    all_to_all x1, blocking collectives, shards(): lax.all_to_all(pieces, ('az', 'ax', 'obs'), split_axis=0, concat_axis=0,...  19.8 us
    pallas_call x1, Pallas kernels, shards(): pl.pallas_call(body, out_shape=pltpu.VMEM((az_count * ax_count * 8, 128),...  8.02 us
    concatenate x1, other arithmetic, shards(): return jnp.concatenate([total[:, :64], total[:, 64:]], axis=0)  0.6 us

profile of v5, /device:TPU:2, one launch (start us, length us, event | category | flops | bytes accessed | tf_op | source)
XLA Modules:
  0.0 28.6 jit_solution(3961053848256810418)
XLA Ops:
  0.0 8.0 %far_field.1 = bf16[512,128]{1,0:T(8,128)(2,1)S(1)} custom-call(s32[1024]{0:T(1024)} %refs_0_.1, s32[8]{0:T(128)} %refs_1_.1, s32[1,64]{1,0:T(1,128)} %bitcast.7, bf16[512,256]{1,0:T(8,128)(2,1)} %constant.4.clone.refs_3_, bf16[2048,512]{1,0:T(8,128)(2,1)} %bitcast.5, bf16[2048,512]{1,0:T(8,128)(2,1)} %bitcast.6), custom_call_target="tpu_custom_call" | custom-call | tf_op jit(solution)/shard_map/far_field/pallas_call | solution.py:273
  8.0 19.8 %all_to_all.5 = bf16[64,8,128]{2,1,0:T(8,128)(2,1)S(1)} all-to-all(bf16[64,8,128]{2,1,0:T(8,128)(2,1)S(1)} %bitcast.4), channel_id=1, replica_groups={{202,206,198,194,218,222,214,210,234,238,230,226,250,254,246,242,186,19..., dimensions={0} | all-to-all | bytes 262144 | tf_op jit(solution)/shard_map/all_to_all | solution.py:301
  27.8 0.1 convert_reduce_fusion
  27.9 0.1 fusion
  28.0 0.6 %pad_maximum_fusion = f32[16,64]{1,0:T(8,128)} fusion(f32[8,64]{1,0:T(8,128)S(1)} %get-tuple-element.6, f32[8,64]{1,0:T(8,128)S(1)} %get-tuple-element.5), kind=kLoop, calls=%fused_computation.1 | loop fusion | flops 1024 | bytes 8192 | tf_op jit(solution)/shard_map/concatenate | solution.py:310

commit v6 on v5

--- a/solution.py
+++ b/solution.py
@@ -12,6 +12,7 @@
 MODES = 64
 POLARS = 32
 ARC_POINTS = 64
+EARLY = 24
 STRIDE = 40
 
 SPACING = 0.1
@@ -152,7 +153,7 @@
         green[p, 2] = ratio * (re * inverse - wave_im)
         green[p, 3] = ratio * (wave_re + im * inverse)
 
-    for p in range(POLARS):
+    for p in range(EARLY):
         polar_step(p)
 
     fetch[1].wait()
@@ -172,9 +173,12 @@
     modal += lax.dot_general(arc_low, ring, contract, preferred_element_type=jnp.float32)
     modal = modal.astype(jnp.bfloat16)
 
-    for copy in fetch[2:5]:
-        copy.wait()
+    fetch[2].wait()
     for f in range(2):
+        fetch[3 + f].wait()
+        if f == 0:
+            for p in range(EARLY, POLARS):
+                polar_step(p)
         for first in range(0, az_rows, 8):
             value = jnp.dot(
                 field[f, first * z_rows : (first + 8) * z_rows],

time: 28.7 us -> 28.3 us (0.986)
  Pallas kernels: 8.02 us -> 7.68 us
    pallas_call x1, Pallas kernels: 8.02 us -> 7.68 us  [shards(): pl.pallas_call(body, out_shape=pltpu.VMEM((az_count * ax_count * 8, 128),...]
where the time goes in v6:
time: 28.3 us; the launch traced here: 28.2 us
  blocking collectives  19.8 us (70%)
  Pallas kernels  7.68 us (27%)
  other arithmetic  0.67 us (2%)
    all_to_all x1, blocking collectives, shards(): lax.all_to_all(pieces, ('az', 'ax', 'obs'), split_axis=0, concat_axis=0,...  19.8 us
    pallas_call x1, Pallas kernels, shards(): pl.pallas_call(body, out_shape=pltpu.VMEM((az_count * ax_count * 8, 128),...  7.68 us
    concatenate x1, other arithmetic, shards(): return jnp.concatenate([total[:, :64], total[:, 64:]], axis=0)  0.6 us

profile of v6, /device:TPU:2, one launch (start us, length us, event | category | flops | bytes accessed | tf_op | source)
XLA Modules:
  0.0 28.2 jit_solution(14624083478352150771)
XLA Ops:
  0.0 7.7 %far_field.1 = bf16[512,128]{1,0:T(8,128)(2,1)S(1)} custom-call(s32[1024]{0:T(1024)} %refs_0_.1, s32[8]{0:T(128)} %refs_1_.1, s32[1,64]{1,0:T(1,128)} %bitcast.7, bf16[512,256]{1,0:T(8,128)(2,1)} %constant.4.clone.refs_3_, bf16[2048,512]{1,0:T(8,128)(2,1)} %bitcast.5, bf16[2048,512]{1,0:T(8,128)(2,1)} %bitcast.6), custom_call_target="tpu_custom_call" | custom-call | tf_op jit(solution)/shard_map/far_field/pallas_call | solution.py:277
  7.7 19.8 %all_to_all.5 = bf16[64,8,128]{2,1,0:T(8,128)(2,1)S(1)} all-to-all(bf16[64,8,128]{2,1,0:T(8,128)(2,1)S(1)} %bitcast.4), channel_id=1, replica_groups={{202,206,198,194,218,222,214,210,234,238,230,226,250,254,246,242,186,19..., dimensions={0} | all-to-all | bytes 262144 | tf_op jit(solution)/shard_map/all_to_all | solution.py:305
  27.5 0.1 convert_reduce_fusion
  27.5 0.1 fusion
  27.6 0.6 %pad_maximum_fusion = f32[16,64]{1,0:T(8,128)} fusion(f32[8,64]{1,0:T(8,128)S(1)} %get-tuple-element.6, f32[8,64]{1,0:T(8,128)S(1)} %get-tuple-element.5), kind=kLoop, calls=%fused_computation.1 | loop fusion | flops 1024 | bytes 8192 | tf_op jit(solution)/shard_map/concatenate | solution.py:314

commit v7 on v6

--- a/solution.py
+++ b/solution.py
@@ -285,10 +285,10 @@
             pltpu.VMEM((1, MODES), jnp.int32),
             pltpu.VMEM(basis.shape, jnp.bfloat16),
             pltpu.VMEM((2, *flat), jnp.bfloat16),
-            pltpu.VMEM((4, az_rows * STRIDE, FREQS), jnp.float32),
-            pltpu.VMEM((4, ARC_POINTS * STRIDE, FREQS), jnp.float32),
+            pltpu.VMEM((4, (az_rows + 1) * STRIDE, FREQS), jnp.float32),
+            pltpu.VMEM((4, (ARC_POINTS + 1) * STRIDE, FREQS), jnp.float32),
             pltpu.VMEM((POLARS, 4, z_rows, FREQS), jnp.float32),
-            pltpu.VMEM((2, observer_ids.shape[0] // obs_count * 8, FREQS), jnp.float32),
+            pltpu.VMEM((2, observer_ids.shape[0] // obs_count * 8 + 8, FREQS), jnp.float32),
             pltpu.SemaphoreType.DMA((6,)),
         ],
         compiler_params=pltpu.CompilerParams(vmem_limit_bytes=60 * 1024 * 1024),

time: 28.3 us -> 28.4 us (level)
  no operation moved by 1% of the time
where the time goes in v7:
time: 28.4 us; the launch traced here: 28.2 us
  blocking collectives  19.8 us (70%)
  Pallas kernels  7.7 us (27%)
  other arithmetic  0.67 us (2%)
    all_to_all x1, blocking collectives, shards(): lax.all_to_all(pieces, ('az', 'ax', 'obs'), split_axis=0, concat_axis=0,...  19.8 us
    pallas_call x1, Pallas kernels, shards(): pl.pallas_call(body, out_shape=pltpu.VMEM((az_count * ax_count * 8, 128),...  7.7 us
    concatenate x1, other arithmetic, shards(): return jnp.concatenate([total[:, :64], total[:, 64:]], axis=0)  0.6 us

profile of v7, /device:TPU:2, one launch (start us, length us, event | category | flops | bytes accessed | tf_op | source)
XLA Modules:
  0.0 28.2 jit_solution(10552064570119612615)
XLA Ops:
  0.0 7.7 %far_field.1 = bf16[512,128]{1,0:T(8,128)(2,1)S(1)} custom-call(s32[1024]{0:T(1024)} %refs_0_.1, s32[8]{0:T(128)} %refs_1_.1, s32[1,64]{1,0:T(1,128)} %bitcast.7, bf16[512,256]{1,0:T(8,128)(2,1)} %constant.4.clone.refs_3_, bf16[2048,512]{1,0:T(8,128)(2,1)} %bitcast.5, bf16[2048,512]{1,0:T(8,128)(2,1)} %bitcast.6), custom_call_target="tpu_custom_call" | custom-call | tf_op jit(solution)/shard_map/far_field/pallas_call | solution.py:277
  7.7 19.8 %all_to_all.5 = bf16[64,8,128]{2,1,0:T(8,128)(2,1)S(1)} all-to-all(bf16[64,8,128]{2,1,0:T(8,128)(2,1)S(1)} %bitcast.4), channel_id=1, replica_groups={{202,206,198,194,218,222,214,210,234,238,230,226,250,254,246,242,186,19..., dimensions={0} | all-to-all | bytes 262144 | tf_op jit(solution)/shard_map/all_to_all | solution.py:305
  27.5 0.1 convert_reduce_fusion
  27.5 0.1 fusion
  27.6 0.6 %pad_maximum_fusion = f32[16,64]{1,0:T(8,128)} fusion(f32[8,64]{1,0:T(8,128)S(1)} %get-tuple-element.6, f32[8,64]{1,0:T(8,128)S(1)} %get-tuple-element.5), kind=kLoop, calls=%fused_computation.1 | loop fusion | flops 1024 | bytes 8192 | tf_op jit(solution)/shard_map/concatenate | solution.py:314

commit v8 on v7

--- a/solution.py
+++ b/solution.py
@@ -173,6 +173,8 @@
     modal += lax.dot_general(arc_low, ring, contract, preferred_element_type=jnp.float32)
     modal = modal.astype(jnp.bfloat16)
 
+    pitch, arc_pitch = az_rows * STRIDE, ARC_POINTS * STRIDE
+    sum_pitch = ids_ref.shape[0] // obs_count * 8
     fetch[2].wait()
     for f in range(2):
         fetch[3 + f].wait()
@@ -187,13 +189,12 @@
             )
             for i in range(8):
                 here = value[i * z_rows : (i + 1) * z_rows]
-                there = pl.ds((first + i) * STRIDE, z_rows)
-                spectrum[2 * f, there] = here[:, :FREQS]
-                spectrum[2 * f + 1, there] = here[:, FREQS:]
+                there = 2 * f * pitch + (first + i) * STRIDE
+                spectrum[pl.ds(there, z_rows)] = here[:, :FREQS]
+                spectrum[pl.ds(there + pitch, z_rows)] = here[:, FREQS:]
 
     def panel_step(z, carry):
-        rows = pl.ds(z, az_rows, stride=STRIDE)
-        parts = [spectrum[c, rows] for c in range(4)]
+        parts = [spectrum[pl.ds(c * pitch + z, az_rows, stride=STRIDE)] for c in range(4)]
         source = jnp.concatenate(
             [
                 jnp.concatenate([parts[0], parts[2]], axis=1),
@@ -202,11 +203,9 @@
             axis=0,
         ).astype(jnp.bfloat16)
         value = jnp.dot(modal, source, preferred_element_type=jnp.float32)
-        there = pl.ds(z, ARC_POINTS, stride=STRIDE)
-        wave[0, there] = value[:64, :128]
-        wave[1, there] = value[64:, :128]
-        wave[2, there] = value[:64, 128:]
-        wave[3, there] = value[64:, 128:]
+        quarters = (value[:64, :128], value[64:, :128], value[:64, 128:], value[64:, 128:])
+        for c, part in enumerate(quarters):
+            wave[pl.ds(c * arc_pitch + z, ARC_POINTS, stride=STRIDE)] = part
         return carry
 
     lax.fori_loop(0, z_rows, panel_step, 0, unroll=8)
@@ -226,14 +225,14 @@
         for j in range(per_block):
             where = ids_ref[first_id + j]
             p, q = where >> 6, where & 63
-            rows = pl.ds(pl.multiple_of(q * STRIDE, 8), z_rows)
+            first = pl.multiple_of(q * STRIDE, 8)
             k0, k1, k2, k3 = (green[p, c] for c in range(4))
-            w0, w1, w2, w3 = (wave[c, rows] for c in range(4))
+            w0, w1, w2, w3 = (wave[pl.ds(c * arc_pitch + first, z_rows)] for c in range(4))
             re = (k0 * w0 - k1 * w1) + (k2 * w2 - k3 * w3)
             im = (k0 * w1 + k1 * w0) + (k2 * w3 + k3 * w2)
-            there = pl.ds(pl.multiple_of((block * per_block + j) * 8, 8), 8)
-            sums[0, there] = jnp.sum(re.reshape(z_rows // 8, 8, 128), axis=0)
-            sums[1, there] = jnp.sum(im.reshape(z_rows // 8, 8, 128), axis=0)
+            there = pl.multiple_of((block * per_block + j) * 8, 8)
+            sums[pl.ds(there, 8)] = jnp.sum(re.reshape(z_rows // 8, 8, 128), axis=0)
+            sums[pl.ds(sum_pitch + there, 8)] = jnp.sum(im.reshape(z_rows // 8, 8, 128), axis=0)
         return carry
 
     lax.fori_loop(0, az_count, observer_step, 0, unroll=4)
@@ -243,8 +242,8 @@
         for part in range(2):
             halves = []
             for half in range(2):
-                first = (block * per_block + half * 8) * 8
-                rows = [sums[part, pl.ds(first + i, 8, stride=8)] for i in range(8)]
+                first = part * sum_pitch + (block * per_block + half * 8) * 8
+                rows = [sums[pl.ds(first + i, 8, stride=8)] for i in range(8)]
                 while len(rows) > 1:
                     rows = [x + y for x, y in zip(rows[::2], rows[1::2])]
                 halves.append(rows[0])
@@ -285,10 +284,10 @@
             pltpu.VMEM((1, MODES), jnp.int32),
             pltpu.VMEM(basis.shape, jnp.bfloat16),
             pltpu.VMEM((2, *flat), jnp.bfloat16),
-            pltpu.VMEM((4, (az_rows + 1) * STRIDE, FREQS), jnp.float32),
-            pltpu.VMEM((4, (ARC_POINTS + 1) * STRIDE, FREQS), jnp.float32),
+            pltpu.VMEM((4 * az_rows * STRIDE + STRIDE, FREQS), jnp.float32),
+            pltpu.VMEM((4 * ARC_POINTS * STRIDE + STRIDE, FREQS), jnp.float32),
             pltpu.VMEM((POLARS, 4, z_rows, FREQS), jnp.float32),
-            pltpu.VMEM((2, observer_ids.shape[0] // obs_count * 8 + 8, FREQS), jnp.float32),
+            pltpu.VMEM((2 * observer_ids.shape[0] // obs_count * 8 + 8, FREQS), jnp.float32),
             pltpu.SemaphoreType.DMA((6,)),
         ],
         compiler_params=pltpu.CompilerParams(vmem_limit_bytes=60 * 1024 * 1024),

time: 28.4 us -> 28.3 us (level)
  no operation moved by 1% of the time
where the time goes in v8:
time: 28.3 us; the launch traced here: 28.2 us
  blocking collectives  19.8 us (70%)
  Pallas kernels  7.68 us (27%)
  other arithmetic  0.67 us (2%)
    all_to_all x1, blocking collectives, shards(): lax.all_to_all(pieces, ('az', 'ax', 'obs'), split_axis=0, concat_axis=0,...  19.8 us
    pallas_call x1, Pallas kernels, shards(): pl.pallas_call(body, out_shape=pltpu.VMEM((az_count * ax_count * 8, 128),...  7.68 us
    concatenate x1, other arithmetic, shards(): return jnp.concatenate([total[:, :64], total[:, 64:]], axis=0)  0.6 us

profile of v8, /device:TPU:2, one launch (start us, length us, event | category | flops | bytes accessed | tf_op | source)
XLA Modules:
  0.0 28.2 jit_solution(1611512501914442619)
XLA Ops:
  0.0 7.7 %far_field.1 = bf16[512,128]{1,0:T(8,128)(2,1)S(1)} custom-call(s32[1024]{0:T(1024)} %refs_0_.1, s32[8]{0:T(128)} %refs_1_.1, s32[1,64]{1,0:T(1,128)} %bitcast.7, bf16[512,256]{1,0:T(8,128)(2,1)} %constant.4.clone.refs_3_, bf16[2048,512]{1,0:T(8,128)(2,1)} %bitcast.5, bf16[2048,512]{1,0:T(8,128)(2,1)} %bitcast.6), custom_call_target="tpu_custom_call" | custom-call | tf_op jit(solution)/shard_map/far_field/pallas_call | solution.py:276
  7.7 19.8 %all_to_all.5 = bf16[64,8,128]{2,1,0:T(8,128)(2,1)S(1)} all-to-all(bf16[64,8,128]{2,1,0:T(8,128)(2,1)S(1)} %bitcast.4), channel_id=1, replica_groups={{202,206,198,194,218,222,214,210,234,238,230,226,250,254,246,242,186,19..., dimensions={0} | all-to-all | bytes 262144 | tf_op jit(solution)/shard_map/all_to_all | solution.py:304
  27.5 0.1 convert_reduce_fusion
  27.5 0.1 fusion
  27.6 0.6 %pad_maximum_fusion = f32[16,64]{1,0:T(8,128)} fusion(f32[8,64]{1,0:T(8,128)S(1)} %get-tuple-element.6, f32[8,64]{1,0:T(8,128)S(1)} %get-tuple-element.5), kind=kLoop, calls=%fused_computation.1 | loop fusion | flops 1024 | bytes 8192 | tf_op jit(solution)/shard_map/concatenate | solution.py:313

commit v9 on v7

--- a/solution.py
+++ b/solution.py
@@ -100,12 +100,16 @@
     modes_ref,
     basis_ref,
     field,
-    spectrum,
-    wave,
+    spectrum0,
+    spectrum1,
+    wave0,
+    wave1,
     green,
-    sums,
+    sums0,
+    sums1,
     sems,
 ):
+    spectrum, wave, sums = (spectrum0, spectrum1), (wave0, wave1), (sums0, sums1)
     fetch = [
         pltpu.make_async_copy(source, target, sems.at[i])
         for i, (source, target) in enumerate(
@@ -173,51 +177,43 @@
     modal += lax.dot_general(arc_low, ring, contract, preferred_element_type=jnp.float32)
     modal = modal.astype(jnp.bfloat16)
 
-    fetch[2].wait()
-    for f in range(2):
-        fetch[3 + f].wait()
-        if f == 0:
-            for p in range(EARLY, POLARS):
-                polar_step(p)
-        for first in range(0, az_rows, 8):
-            value = jnp.dot(
-                field[f, first * z_rows : (first + 8) * z_rows],
-                basis_ref[...],
-                preferred_element_type=jnp.float32,
-            )
-            for i in range(8):
-                here = value[i * z_rows : (i + 1) * z_rows]
-                there = pl.ds((first + i) * STRIDE, z_rows)
-                spectrum[2 * f, there] = here[:, :FREQS]
-                spectrum[2 * f + 1, there] = here[:, FREQS:]
-
-    def panel_step(z, carry):
-        rows = pl.ds(z, az_rows, stride=STRIDE)
-        parts = [spectrum[c, rows] for c in range(4)]
-        source = jnp.concatenate(
-            [
-                jnp.concatenate([parts[0], parts[2]], axis=1),
-                jnp.concatenate([parts[1], parts[3]], axis=1),
-            ],
-            axis=0,
-        ).astype(jnp.bfloat16)
-        value = jnp.dot(modal, source, preferred_element_type=jnp.float32)
-        there = pl.ds(z, ARC_POINTS, stride=STRIDE)
-        wave[0, there] = value[:64, :128]
-        wave[1, there] = value[64:, :128]
-        wave[2, there] = value[:64, 128:]
-        wave[3, there] = value[64:, 128:]
-        return carry
-
-    lax.fori_loop(0, z_rows, panel_step, 0, unroll=8)
-
-    fetch[5].wait()
     lane = lax.broadcasted_iota(jnp.int32, (8, 128), 1)
     per_block = ids_ref.shape[0] // (az_count * obs_count)
     z_count = az_count // 2
     twist = (obs >> 1) ^ (az // z_count)
 
-    def observer_step(block, carry):
+    def time_chunk(f, first):
+        value = jnp.dot(
+            field[f, first * z_rows : (first + 8) * z_rows],
+            basis_ref[...],
+            preferred_element_type=jnp.float32,
+        )
+        for i in range(8):
+            here = value[i * z_rows : (i + 1) * z_rows]
+            there = pl.ds((first + i) * STRIDE, z_rows)
+            spectrum[f][0, there] = here[:, :FREQS]
+            spectrum[f][1, there] = here[:, FREQS:]
+
+    def panel_pairs(f):
+        def pair_step(i, carry):
+            parts = [
+                [spectrum[f][c, pl.ds(2 * i + k, az_rows, stride=STRIDE)] for k in range(2)]
+                for c in range(2)
+            ]
+            source = jnp.concatenate(
+                [jnp.concatenate(part, axis=1) for part in parts], axis=0
+            ).astype(jnp.bfloat16)
+            value = jnp.dot(modal, source, preferred_element_type=jnp.float32)
+            for k in range(2):
+                there = pl.ds(2 * i + k, ARC_POINTS, stride=STRIDE)
+                columns = value[:, k * FREQS : (k + 1) * FREQS]
+                wave[f][0, there] = columns[:64]
+                wave[f][1, there] = columns[64:]
+            return carry
+
+        lax.fori_loop(0, z_rows // 2, pair_step, 0, unroll=8)
+
+    def observers(f, block):
         y = 1 - block // z_count
         z = block % z_count
         z = jnp.where(z < z_count // 2, z + z_count // 2, z_count - 1 - z)
@@ -227,13 +223,31 @@
             where = ids_ref[first_id + j]
             p, q = where >> 6, where & 63
             rows = pl.ds(pl.multiple_of(q * STRIDE, 8), z_rows)
-            k0, k1, k2, k3 = (green[p, c] for c in range(4))
-            w0, w1, w2, w3 = (wave[c, rows] for c in range(4))
-            re = (k0 * w0 - k1 * w1) + (k2 * w2 - k3 * w3)
-            im = (k0 * w1 + k1 * w0) + (k2 * w3 + k3 * w2)
+            k0, k1 = green[p, 2 * f], green[p, 2 * f + 1]
+            w0, w1 = wave[f][0, rows], wave[f][1, rows]
+            re = k0 * w0 - k1 * w1
+            im = k0 * w1 + k1 * w0
             there = pl.ds(pl.multiple_of((block * per_block + j) * 8, 8), 8)
-            sums[0, there] = jnp.sum(re.reshape(z_rows // 8, 8, 128), axis=0)
-            sums[1, there] = jnp.sum(im.reshape(z_rows // 8, 8, 128), axis=0)
+            sums[f][0, there] = jnp.sum(re.reshape(z_rows // 8, 8, 128), axis=0)
+            sums[f][1, there] = jnp.sum(im.reshape(z_rows // 8, 8, 128), axis=0)
+
+    fetch[2].wait()
+    fetch[3].wait()
+    for p in range(EARLY, POLARS):
+        polar_step(p)
+    for first in range(0, az_rows, 8):
+        time_chunk(0, first)
+    panel_pairs(0)
+    fetch[4].wait()
+    fetch[5].wait()
+    for first in range(0, az_rows, 8):
+        time_chunk(1, first)
+        observers(0, first // 4)
+        observers(0, first // 4 + 1)
+    panel_pairs(1)
+
+    def observer_step(block, carry):
+        observers(1, block)
         return carry
 
     lax.fori_loop(0, az_count, observer_step, 0, unroll=4)
@@ -244,7 +258,7 @@
             halves = []
             for half in range(2):
                 first = (block * per_block + half * 8) * 8
-                rows = [sums[part, pl.ds(first + i, 8, stride=8)] for i in range(8)]
+                rows = [sums[f][part, pl.ds(first + i, 8, stride=8)] for f in range(2) for i in range(8)]
                 while len(rows) > 1:
                     rows = [x + y for x, y in zip(rows[::2], rows[1::2])]
                 halves.append(rows[0])
@@ -285,9 +299,12 @@
             pltpu.VMEM((1, MODES), jnp.int32),
             pltpu.VMEM(basis.shape, jnp.bfloat16),
             pltpu.VMEM((2, *flat), jnp.bfloat16),
-            pltpu.VMEM((4, (az_rows + 1) * STRIDE, FREQS), jnp.float32),
-            pltpu.VMEM((4, (ARC_POINTS + 1) * STRIDE, FREQS), jnp.float32),
+            pltpu.VMEM((2, (az_rows + 1) * STRIDE, FREQS), jnp.float32),
+            pltpu.VMEM((2, (az_rows + 1) * STRIDE, FREQS), jnp.float32),
+            pltpu.VMEM((2, (ARC_POINTS + 1) * STRIDE, FREQS), jnp.float32),
+            pltpu.VMEM((2, (ARC_POINTS + 1) * STRIDE, FREQS), jnp.float32),
             pltpu.VMEM((POLARS, 4, z_rows, FREQS), jnp.float32),
+            pltpu.VMEM((2, observer_ids.shape[0] // obs_count * 8 + 8, FREQS), jnp.float32),
             pltpu.VMEM((2, observer_ids.shape[0] // obs_count * 8 + 8, FREQS), jnp.float32),
             pltpu.SemaphoreType.DMA((6,)),
         ],

time: 28.4 us -> 28.1 us (0.989)
  no operation moved by 1% of the time
where the time goes in v9:
time: 28.1 us; the launch traced here: 28 us
  blocking collectives  19.8 us (70%)
  Pallas kernels  7.44 us (26%)
  other arithmetic  0.67 us (2%)
    all_to_all x1, blocking collectives, shards(): lax.all_to_all(pieces, ('az', 'ax', 'obs'), split_axis=0, concat_axis=0,...  19.8 us
    pallas_call x1, Pallas kernels, shards(): pl.pallas_call(body, out_shape=pltpu.VMEM((az_count * ax_count * 8, 128),...  7.44 us
    concatenate x1, other arithmetic, shards(): return jnp.concatenate([total[:, :64], total[:, 64:]], axis=0)  0.6 us

profile of v9, /device:TPU:2, one launch (start us, length us, event | category | flops | bytes accessed | tf_op | source)
XLA Modules:
  0.0 28.0 jit_solution(10105847867970219494)
XLA Ops:
  0.0 7.4 %far_field.1 = bf16[512,128]{1,0:T(8,128)(2,1)S(1)} custom-call(s32[1024]{0:T(1024)} %refs_0_.1, s32[8]{0:T(128)} %refs_1_.1, s32[1,64]{1,0:T(1,128)} %bitcast.7, bf16[512,256]{1,0:T(8,128)(2,1)} %constant.4.clone.refs_3_, bf16[2048,512]{1,0:T(8,128)(2,1)} %bitcast.5, bf16[2048,512]{1,0:T(8,128)(2,1)} %bitcast.6), custom_call_target="tpu_custom_call" | custom-call | tf_op jit(solution)/shard_map/far_field/pallas_call | solution.py:291
  7.4 19.8 %all_to_all.5 = bf16[64,8,128]{2,1,0:T(8,128)(2,1)S(1)} all-to-all(bf16[64,8,128]{2,1,0:T(8,128)(2,1)S(1)} %bitcast.4), channel_id=1, replica_groups={{202,206,198,194,218,222,214,210,234,238,230,226,250,254,246,242,186,19..., dimensions={0} | all-to-all | bytes 262144 | tf_op jit(solution)/shard_map/all_to_all | solution.py:322
  27.2 0.1 convert_reduce_fusion
  27.3 0.1 fusion
  27.3 0.6 %pad_maximum_fusion = f32[16,64]{1,0:T(8,128)} fusion(f32[8,64]{1,0:T(8,128)S(1)} %get-tuple-element.6, f32[8,64]{1,0:T(8,128)S(1)} %get-tuple-element.5), kind=kLoop, calls=%fused_computation.1 | loop fusion | flops 1024 | bytes 8192 | tf_op jit(solution)/shard_map/concatenate | solution.py:331

commit v10 on v9

--- a/solution.py
+++ b/solution.py
@@ -13,7 +13,7 @@
 POLARS = 32
 ARC_POINTS = 64
 EARLY = 24
-STRIDE = 40
+STRIDE = 56
 
 SPACING = 0.1
 RADIUS = 1.0

time: 28.1 us -> 28.1 us (level)
  no operation moved by 1% of the time
where the time goes in v10:
time: 28.1 us; the launch traced here: 28 us
  blocking collectives  19.8 us (70%)
  Pallas kernels  7.45 us (27%)
  other arithmetic  0.67 us (2%)
    all_to_all x1, blocking collectives, shards(): lax.all_to_all(pieces, ('az', 'ax', 'obs'), split_axis=0, concat_axis=0,...  19.8 us
    pallas_call x1, Pallas kernels, shards(): pl.pallas_call(body, out_shape=pltpu.VMEM((az_count * ax_count * 8, 128),...  7.45 us
    concatenate x1, other arithmetic, shards(): return jnp.concatenate([total[:, :64], total[:, 64:]], axis=0)  0.6 us

profile of v10, /device:TPU:2, one launch (start us, length us, event | category | flops | bytes accessed | tf_op | source)
XLA Modules:
  0.0 28.0 jit_solution(10332383229381276519)
XLA Ops:
  0.0 7.5 %far_field.1 = bf16[512,128]{1,0:T(8,128)(2,1)S(1)} custom-call(s32[1024]{0:T(1024)} %refs_0_.1, s32[8]{0:T(128)} %refs_1_.1, s32[1,64]{1,0:T(1,128)} %bitcast.7, bf16[512,256]{1,0:T(8,128)(2,1)} %constant.4.clone.refs_3_, bf16[2048,512]{1,0:T(8,128)(2,1)} %bitcast.5, bf16[2048,512]{1,0:T(8,128)(2,1)} %bitcast.6), custom_call_target="tpu_custom_call" | custom-call | tf_op jit(solution)/shard_map/far_field/pallas_call | solution.py:291
  7.5 19.8 %all_to_all.5 = bf16[64,8,128]{2,1,0:T(8,128)(2,1)S(1)} all-to-all(bf16[64,8,128]{2,1,0:T(8,128)(2,1)S(1)} %bitcast.4), channel_id=1, replica_groups={{202,206,198,194,218,222,214,210,234,238,230,226,250,254,246,242,186,19..., dimensions={0} | all-to-all | bytes 262144 | tf_op jit(solution)/shard_map/all_to_all | solution.py:322
  27.2 0.1 convert_reduce_fusion
  27.3 0.1 fusion
  27.4 0.6 %pad_maximum_fusion = f32[16,64]{1,0:T(8,128)} fusion(f32[8,64]{1,0:T(8,128)S(1)} %get-tuple-element.6, f32[8,64]{1,0:T(8,128)S(1)} %get-tuple-element.5), kind=kLoop, calls=%fused_computation.1 | loop fusion | flops 1024 | bytes 8192 | tf_op jit(solution)/shard_map/concatenate | solution.py:331
